TPU v7x, 256 devices: a whole 4x4x8 slice. The times are simulated.
256 devices in a mesh: row: 32 (over y, x, core), col: 8 (over z).
Axes of the slice: x: 4, y: 4, z: 8, core: 2. Of those that a mesh axis runs over, the one named last changes fastest.
Arguments:
- tiles: bfloat16 [32, 8, 48, 256, 256], P('row', 'col'), may hold values from -6 to 6
- coords: int32 [32, 8, 48, 2], P('row', 'col'), may hold values from 0 to 7, as said below
- counts: int32 [32, 8], P('row', 'col'), may hold values from 8 to 48, as said below
- panel: bfloat16 [65536, 512], P(('row', 'col')), may hold values from -6 to 6
Outputs:
- basis: float32 [16384, 512], P(('col', 'row'))
Inputs may be any that keep to these rules, and one draw needn't show every extreme that they name: `coords`: on each device the first counts slots name distinct positions, block row below 8 and block column below 8; later slots name valid positions too. `counts`: some device holds 48 live tiles in every draw.
All inputs are finite; a program needn't handle non-finite values.
Results may differ from a plain program's by a relative error of at most 0.0003.
Values may be sent and summed in bfloat16 or wider, within the bound.
A program may use at most 128 MiB of HBM per device.

v0:
```python
import jax
import jax.numpy as jnp
from jax import lax
from jax.sharding import PartitionSpec as P

CB_DEV = 8


def local(tiles, coords, counts, panel):
    hi = lax.Precision.HIGHEST
    gathered = lax.all_gather(panel, "col", axis=0, tiled=True)
    values = tiles[0, 0]
    where = coords[0, 0]
    live_count = counts[0, 0]
    edge = values.shape[1]
    width = gathered.shape[1]
    col_blocks = CB_DEV

    def add_tile(slot, total):
        block_row = where[slot, 0]
        block_col = where[slot, 1]
        single = lax.dynamic_index_in_dim(values, slot, 0, keepdims=False)
        rows_in = lax.dynamic_slice_in_dim(gathered, block_row * edge, edge, 0)
        term = lax.dot_general(
            single, rows_in, (((0,), (0,)), ((), ())), preferred_element_type=jnp.float32
        )
        current = lax.dynamic_slice_in_dim(total, block_col * edge, edge, 0)
        return lax.dynamic_update_slice_in_dim(total, current + term, block_col * edge, 0)

    start = jnp.zeros((col_blocks * edge, width), jnp.float32)
    partial_sum = lax.fori_loop(0, live_count, add_tile, start)
    total_cols = partial_sum.shape[0] * lax.axis_size("col")
    own_rows = lax.psum_scatter(partial_sum, "row", scatter_dimension=0, tiled=True)
    local_gram = lax.dot_general(
        own_rows,
        own_rows,
        (((0,), (0,)), ((), ())),
        precision=hi,
        preferred_element_type=jnp.float32,
    )
    gram = lax.psum(local_gram, ("row", "col"))
    lower = jnp.linalg.cholesky(gram)
    solved = jax.scipy.linalg.solve_triangular(lower, own_rows.T, lower=True)
    return solved.T * jnp.sqrt(jnp.float32(total_cols))


def solution(mesh):
    placed = (
        P("row", "col", None, None, None),
        P("row", "col", None, None),
        P("row", "col"),
        P(("row", "col"), None),
    )
    return jax.shard_map(
        local, mesh=mesh, in_specs=placed, out_specs=P(("col", "row"), None), check_vma=False
    )
```

profile of v0, /device:TPU:1, one launch (start us, length us, event | category | flops | bytes accessed | tf_op | source)
XLA Modules:
  0.0 777.1 jit_solution(12633065833763122414)
XLA Ops:
  6.5 0.7 all-gather.2.cloned.1.call-update
  7.3 43.1 %all-gather.2.cloned.1.call-done = bf16[2048,512]{1,0:T(8,128)(2,1)} async-done(((bf16[256,512]{1,0:T(8,128)(2,1)}), bf16[2048,512]{1,0:T(8,128)(2,1)}) %all-gather.2.cloned.1.call-update) | async-done | bytes 2097168 | tf_op jit(solution)/shard_map/all_gather | solution.py:11
  50.4 2.5 broadcast_in_dim.5
  52.8 39.0 %while.11 = (s32[]{:T(128)}, f32[2048,512]{1,0:T(8,128)}, s32[]{:T(128)}, s32[48,2]{0,1:T(2,128)S(1)}, bf16[48,256,256]{2,1,0:T(8,128)(2,1)}, /*index=5*/bf16[20...) while((s32[]{:T(128)}, f32[2048,512]{1,0:T(8,128)}, ...), condition=%wide.region_1.2_spmd, body=%wide.region_0.1_spmd.sunk | while | flops 67239952 | bytes 1442059 | solution.py:31
  55.4 2.2 fusion.51
  60.2 2.3 fusion.51
  65.0 2.3 fusion.51
  69.8 2.3 fusion.51
  74.6 2.3 fusion.51
  79.4 2.3 fusion.51
  84.1 2.3 fusion.51
  88.9 2.3 fusion.51
  91.9 280.3 %reduce-scatter.2.cloned.1.call-done = f32[64,512]{1,0:T(8,128)} async-done(((f32[2048,512]{1,0:T(8,128)}), f32[64,512]{1,0:T(8,128)}) %reduce-scatter.2.cloned.1.call-update) | async-done | bytes 131088 | tf_op jit(solution)/shard_map/reduce_scatter | solution.py:33
  372.3 3.0 fusion.37
  375.4 258.7 %all-reduce.3.cloned.1.call-done = f32[512,512]{0,1:T(8,128)} async-done(((f32[512,512]{0,1:T(8,128)}), f32[512,512]{0,1:T(8,128)}) %all-reduce.3.cloned.1.call-update) | async-done | bytes 1048592 | tf_op jit(solution)/shard_map/psum | solution.py:41
  634.1 1.6 copy.6
  635.7 1.4 fusion.5
  637.1 11.7 %cholesky.104 = f32[128,128]{1,0:T(8,128)S(1)} custom-call(f32[128,128]{1,0:T(8,128)S(1)} %cholesky.266), custom_call_target="Cholesky" | custom-call | tf_op jit(solution)/shard_map/jit(cholesky)/cholesky | solution.py:42
  649.0 9.8 %custom-call.31 = f32[1,128,128]{1,2,0:T(8,128)S(1)} custom-call(f32[1,128,128]{2,1,0:T(8,128)S(1)} %get-tuple-element.80), custom_call_target="InvertDiagBlocksLowerTriangular" | custom-call | tf_op jit(solution)/shard_map/jit(cholesky)/cholesky | solution.py:42
  659.5 11.7 %cholesky.217 = f32[128,128]{1,0:T(8,128)S(1)} custom-call(f32[128,128]{1,0:T(8,128)S(1)} %cholesky.270), custom_call_target="Cholesky" | custom-call | tf_op jit(solution)/shard_map/jit(cholesky)/cholesky | solution.py:42
  671.3 9.9 %custom-call.32 = f32[1,128,128]{1,2,0:T(8,128)S(1)} custom-call(f32[1,128,128]{2,1,0:T(8,128)S(1)} %get-tuple-element.77), custom_call_target="InvertDiagBlocksLowerTriangular" | custom-call | tf_op jit(solution)/shard_map/jit(cholesky)/cholesky | solution.py:42
  681.9 11.7 %cholesky.238 = f32[128,128]{1,0:T(8,128)S(1)} custom-call(f32[128,128]{1,0:T(8,128)S(1)} %cholesky.275), custom_call_target="Cholesky" | custom-call | tf_op jit(solution)/shard_map/jit(cholesky)/cholesky | solution.py:42
  693.6 0.7 compare_reduce_fusion.1
  694.3 9.8 %custom-call.33 = f32[1,128,128]{1,2,0:T(8,128)S(1)} custom-call(f32[1,128,128]{2,1,0:T(8,128)S(1)} %get-tuple-element.74), custom_call_target="InvertDiagBlocksLowerTriangular" | custom-call | tf_op jit(solution)/shard_map/jit(cholesky)/cholesky | solution.py:42
  704.7 11.9 %cholesky.255 = f32[128,128]{1,0:T(8,128)S(1)} custom-call(f32[128,128]{1,0:T(8,128)S(1)} %convolution_subtract_fusion.2), custom_call_target="Cholesky" | custom-call | tf_op jit(solution)/shard_map/jit(cholesky)/cholesky | solution.py:42
  717.3 0.7 compare_reduce_fusion.2
  720.7 8.1 %while.12 = (s32[]{:T(128)}, f32[512,512]{1,0:T(8,128)S(1)}, s32[4,2]{0,1:T(2,128)S(1)}, f32[4,128,128]{2,1,0:T(8,128)S(1)}, s32[]{:T(128)}) while((s32[]{:T(128)}, f32[512,512]{1,0:T(8,128)S(1)}, s32[4,2]{0,1:T(2,128)S(1)}, f32[4,128,128]{2,1,0:T(8,128)S(1)}, s32[]{:T(128)}) %tuple.46), condition=%wide.while_cond, body=%wide.while_body.sunk | while | flops 2 | bytes 131181 | solution.py:43
  721.4 1.3 bitcast_dynamic-update-slice_fusion.2
  723.4 1.3 bitcast_dynamic-update-slice_fusion.2
  725.5 1.3 bitcast_dynamic-update-slice_fusion.2
  727.5 1.3 bitcast_dynamic-update-slice_fusion.2
  728.8 39.3 %custom-call.34 = f32[4,128,128]{1,2,0:T(8,128)S(1)} custom-call(f32[4,128,128]{2,1,0:T(8,128)S(1)} %get-tuple-element.46), custom_call_target="InvertDiagBlocksLowerTriangular" | custom-call | tf_op jit(solution)/shard_map/jit(_solve_triangular)/triangular_solve | solution.py:43
  (52 shorter events, 13.3 us)
Async XLA Ops:
  6.5 46.3 %copy-start.1 = (s32[1,1,48,2]{2,3,1,0:T(2,128)S(1)}, s32[1,1,48,2]{2,3,1,0:T(2,128)}, u32[]{:S(2)}) copy-start(s32[1,1,48,2]{2,3,1,0:T(2,128)} %param.7) | copy-start | bytes 1156
  6.5 43.8 %all-gather.2.cloned.1.call-start = ((), (), s32[]{:S(2)}) async-start(), calls=%async_computation.1 | async-start | bytes 2359296 | tf_op jit(solution)/shard_map/all_gather | solution.py:11
  7.3 365.0 %reduce-scatter.2.cloned.1.call-start = ((), (), s32[]{:S(2)}) async-start(), calls=%async_computation.2 | async-start | bytes 4325376 | tf_op jit(solution)/shard_map/reduce_scatter | solution.py:33
  91.9 542.2 %all-reduce.3.cloned.1.call-start = ((), (), s32[]{:S(2)}) async-start(), calls=%async_computation.3 | async-start | bytes 2097152 | tf_op jit(solution)/shard_map/psum | solution.py:41
  637.1 131.1 %copy-start = (f32[64,512]{1,0:T(8,128)S(1)}, f32[64,512]{1,0:T(8,128)}, u32[]{:S(2)}) copy-start(f32[64,512]{1,0:T(8,128)} %reduce-scatter.2.cloned.1.call-done) | copy-start | bytes 393220
Sparse Core Ops, SparseCore 0:
  9.1 41.1 all-gather.1
  92.0 280.2 reduce-scatter.1
  378.6 255.4 all-reduce.2
where the time goes:
time: 780 us; the launch traced here: 777 us
  waiting for transfers between devices  583 us (75%)
  other arithmetic  120 us (15%)
  matrix products  24.6 us (3%)
  local copies, waits for them, and re-layouts  17.4 us (2%)
  between operations  15.9 us (2%)
  loops' own time  15.8 us (2%)
    reduce_scatter x1, waiting for transfers between devices, local(): lax.psum_scatter(partial_sum, 'row', scatter_dimension=0, tiled=True)  280 us
    psum x1, waiting for transfers between devices, local(): gram = lax.psum(local_gram, ('row', 'col'))  259 us
    another operation x14, other arithmetic, local(): lower = jnp.linalg.cholesky(gram)  78.8 us
    all_gather x1, waiting for transfers between devices, local(): gathered = lax.all_gather(panel, 'col', axis=0, tiled=True)  43.1 us
    another operation x3, other arithmetic, local(): solved = jax.scipy.linalg.solve_triangular(lower, own_rows.T, lower=True)  39.4 us
    dot_general x8, matrix products, add_tile(): lax.dot_general(single, rows_in, (((0,), (0,)), ((), ())), preferred_elem...  18.1 us
    another operation x1, loops' own time, local(): partial_sum = lax.fori_loop(0, live_count, add_tile, start)  15.7 us
  transfers between devices with their start and end apart: 3, of which 3 were waited for; matrix products, arithmetic and copies ran while one was open for 0% of the time, Pallas kernels for 0%

commit v1 on v0

v1 whole, which is shorter than its diff:
```python
import jax
import jax.numpy as jnp
from jax import lax
from jax.experimental import pallas as pl
from jax.experimental.pallas import tpu as pltpu
from jax.sharding import PartitionSpec as P

F32 = jnp.float32
BF16 = jnp.bfloat16
HI = lax.Precision.HIGHEST
TILE = 256
NB = 8
K = 512
SLOTS = 48
VMEM = pltpu.VMEM
SMEM = pltpu.SMEM


def mm(a, b, dims):
    return lax.dot_general(a, b, (dims, ((), ())), precision=HI, preferred_element_type=F32)


def tile_kernel(slot_ref, tiles_hbm, panel_ref, out_ref, tiles_ref, at_ref, sem):
    copy = pltpu.make_async_copy(tiles_hbm, tiles_ref, sem)
    copy.start()
    copy.wait()

    def build(pos, carry):
        slot = slot_ref[pos]
        tile = tiles_ref[jnp.minimum(slot, SLOTS - 1)]
        tile = jnp.where(slot < SLOTS, tile.astype(F32), 0.0).T.astype(BF16)
        block_row, block_col = pos // NB, pos % NB
        at_ref[block_row, pl.ds(pl.multiple_of(block_col * TILE, TILE), TILE), :] = tile
        return carry

    lax.fori_loop(0, NB * NB, build, 0)

    def multiply(col, carry):
        rows = pl.ds(pl.multiple_of(col * TILE, TILE), TILE)
        total = jnp.zeros((TILE, K), F32)
        for b in range(NB):
            total += jnp.dot(
                at_ref[b, rows, :],
                panel_ref[b * TILE:(b + 1) * TILE, :],
                preferred_element_type=F32,
            )
        out_ref[rows, :] = total
        return carry

    lax.fori_loop(0, NB, multiply, 0)


def tile_product(slot_of, tiles, panel):
    return pl.pallas_call(
        tile_kernel,
        out_shape=jax.ShapeDtypeStruct((NB * TILE, K), F32),
        in_specs=[
            pl.BlockSpec(memory_space=SMEM),
            pl.BlockSpec(memory_space=pl.ANY),
            pl.BlockSpec(memory_space=VMEM),
        ],
        out_specs=pl.BlockSpec(memory_space=VMEM),
        scratch_shapes=[
            VMEM((SLOTS, TILE, TILE), BF16),
            VMEM((NB, NB * TILE, TILE), BF16),
            pltpu.SemaphoreType.DMA,
        ],
        compiler_params=pltpu.CompilerParams(vmem_limit_bytes=40 * 2**20),
        name="tile_product",
    )(slot_of, tiles, panel)


def factor(w_ref, b):
    n = 128
    sub = lax.broadcasted_iota(jnp.int32, (b, 128), 0)
    for c0 in range(0, n, b):
        left = w_ref[c0:c0 + b, :128]
        right = w_ref[c0:c0 + b, 128:]
        cols = [jnp.broadcast_to(left[:, c0 + j:c0 + j + 1], (b, 128)) for j in range(b)]
        pivots = jnp.ones((b, 128), F32)
        for j in range(b):
            pivot = cols[j][j:j + 1, :]
            f = jnp.where(sub > j, cols[j] * (1.0 / pivot), 0.0)
            for m in range(j + 1, b):
                cols[m] = cols[m] - f * cols[m][j:j + 1, :]
            if j < b - 1:
                left = left - f * left[j:j + 1, :]
                right = right - f * right[j:j + 1, :]
            pivots = jnp.where(sub == j, pivot, pivots)
        norm = lax.rsqrt(pivots)
        left = left * norm
        right = right * norm
        w_ref[c0:c0 + b, :128] = left
        w_ref[c0:c0 + b, 128:] = right
        e = c0 + b
        if e < n:
            both = jnp.concatenate([left, right], axis=1)
            t = mm(left, both, ((0,), (0,)))
            w_ref[e:, :] = w_ref[e:, :] - t[e:, :]


def basis_kernel(scale, gram_ref, rows_ref, out_ref, s_ref, w_ref):
    eye = (
        lax.broadcasted_iota(jnp.int32, (128, 128), 0)
        == lax.broadcasted_iota(jnp.int32, (128, 128), 1)
    ).astype(F32)
    s_ref[...] = gram_ref[...]
    out_ref[...] = rows_ref[...]
    for i in range(K // 128):
        lo, hi = i * 128, (i + 1) * 128
        w_ref[:, :128] = s_ref[lo:hi, lo:hi]
        w_ref[:, 128:] = eye
        factor(w_ref, 16)
        inv = w_ref[:, 128:]
        x = mm(out_ref[:, lo:hi], inv, ((1,), (1,)))
        out_ref[:, lo:hi] = x * scale
        if hi < K:
            u = mm(inv, s_ref[lo:hi, hi:], ((1,), (0,)))
            s_ref[hi:, hi:] = s_ref[hi:, hi:] - mm(u, u, ((0,), (0,)))
            out_ref[:, hi:] = out_ref[:, hi:] - mm(x, u, ((1,), (0,)))


def cholesky_basis(gram, rows, scale):
    return pl.pallas_call(
        lambda *refs: basis_kernel(scale, *refs),
        out_shape=jax.ShapeDtypeStruct(rows.shape, F32),
        in_specs=[pl.BlockSpec(memory_space=VMEM)] * 2,
        out_specs=pl.BlockSpec(memory_space=VMEM),
        scratch_shapes=[VMEM((K, K), F32), VMEM((128, 256), F32)],
        compiler_params=pltpu.CompilerParams(vmem_limit_bytes=40 * 2**20),
        name="cholesky_basis",
    )(gram, rows)


def local(tiles, coords, counts, panel):
    where = coords[0, 0]
    position = where[:, 0] * NB + where[:, 1]
    slots = jnp.arange(SLOTS, dtype=jnp.int32)
    live = slots < counts[0, 0]
    match = (position[None, :] == jnp.arange(NB * NB, dtype=jnp.int32)[:, None]) & live[None, :]
    slot_of = jnp.min(jnp.where(match, slots[None, :], SLOTS), axis=1)

    gathered = lax.all_gather(panel, "col", axis=0, tiled=True)
    partial_sum = tile_product(slot_of, tiles[0, 0], gathered)
    own_rows = lax.psum_scatter(partial_sum, "row", scatter_dimension=0, tiled=True)
    local_gram = mm(own_rows, own_rows, ((0,), (0,)))
    gram = lax.psum(local_gram, ("row", "col"))
    scale = float((partial_sum.shape[0] * 8) ** 0.5)
    return cholesky_basis(gram, own_rows, scale)


def solution(mesh):
    placed = (
        P("row", "col", None, None, None),
        P("row", "col", None, None),
        P("row", "col"),
        P(("row", "col"), None),
    )
    return jax.shard_map(
        local, mesh=mesh, in_specs=placed, out_specs=P(("col", "row"), None), check_vma=False
    )
```

time: 780 us -> 455 us (0.58)
  waiting for transfers between devices: 583 us -> 391 us
  other arithmetic: 120 us -> 0.86 us
  Pallas kernels: 0 us -> 36.9 us
  matrix products: 24.6 us -> 3.03 us
  loops' own time: 15.8 us -> 0 us
  local copies, waits for them, and re-layouts: 17.4 us -> 8.43 us
    reduce_scatter x1, waiting for transfers between devices: 280 us -> 90.3 us  [local(): lax.psum_scatter(partial_sum, 'row', scatter_dimension=0, tiled=True)]
    another operation x17 -> x0, other arithmetic: 118 us -> none  [the longest x14 78.8 us: local(): lower = jnp.linalg.cholesky(gram)]
    pallas_call x0 -> x2, Pallas kernels: none -> 36.9 us  [the longest x1 23.5 us: cholesky_basis(): pl.pallas_call(lambda *refs: basis_kernel(scale, *refs), out_shape=jax.Sh...]
    dot_general x9 -> x1, matrix products: 21.1 us -> 3.03 us  [mm(): lax.dot_general(a, b, (dims, ((), ())), precision=HI, preferred_element_t...]
    another operation x2 -> x0, loops' own time: 15.8 us -> none  [the longest x1 15.7 us: local(): partial_sum = lax.fori_loop(0, live_count, add_tile, start)]
    unnamed x4 -> x10, local copies, waits for them, and re-layouts: 0.01 us -> 8.43 us
    another operation x17 -> x0, local copies, waits for them, and re-layouts: 8.21 us -> none
where the time goes in v1:
time: 455 us; the launch traced here: 454 us
  waiting for transfers between devices  391 us (86%)
  Pallas kernels  36.9 us (8%)
  between operations  13.8 us (3%)
  local copies, waits for them, and re-layouts  8.43 us (2%)
    psum x1, waiting for transfers between devices, local(): gram = lax.psum(local_gram, ('row', 'col'))  259 us
    reduce_scatter x1, waiting for transfers between devices, local(): lax.psum_scatter(partial_sum, 'row', scatter_dimension=0, tiled=True)  90.3 us
    all_gather x1, waiting for transfers between devices, local(): gathered = lax.all_gather(panel, 'col', axis=0, tiled=True)  41.6 us
    pallas_call x1, Pallas kernels, cholesky_basis(): pl.pallas_call(lambda *refs: basis_kernel(scale, *refs), out_shape=jax.Sh...  23.5 us
    pallas_call x1, Pallas kernels, tile_product(): pl.pallas_call(tile_kernel, out_shape=jax.ShapeDtypeStruct((NB * TILE, K)...  13.4 us
  transfers between devices with their start and end apart: 3, of which 3 were waited for; matrix products, arithmetic and copies ran while one was open for 0% of the time, Pallas kernels for 0%

profile of v1, /device:TPU:1, one launch (start us, length us, event | category | flops | bytes accessed | tf_op | source)
XLA Modules:
  0.0 454.4 jit_solution(13988094898607436595)
XLA Ops:
  6.5 0.0 all-gather.2.cloned.1.call-start
  6.5 0.7 all-gather.2.cloned.1.call-update
  7.3 0.0 reduce-scatter.2.cloned.1.call-start
  8.0 0.8 add_bitcast_fusion
  8.7 0.1 select_reduce_fusion.slot_ref
  8.8 41.6 %all-gather.2.cloned.1.call-done.panel_ref = bf16[2048,512]{1,0:T(8,128)(2,1)} async-done(((bf16[256,512]{1,0:T(8,128)(2,1)}), bf16[2048,512]{1,0:T(8,128)(2,1)}) %all-gather.2.cloned.1.call-update) | async-done | bytes 2097168 | tf_op jit(solution)/shard_map/all_gather | solution.py:143
  50.4 0.0 copy-start.1
  50.4 2.8 copy-done.1
  53.2 0.0 copy-start.2
  53.2 1.6 copy-done.2
  54.8 13.4 %tile_product.1 = f32[2048,512]{1,0:T(8,128)S(1)} custom-call(s32[64]{0:T(128)S(1)} %select_reduce_fusion.slot_ref, bf16[48,256,256]{2,1,0:T(8,128)(2,1)S(1)} %bitcast.8, bf16[2048,512]{1,0:T(8,128)(2,1)S(1)} %copy-done.2), custom_call_target="tpu_custom_call" | custom-call | tf_op jit(solution)/shard_map/tile_product/pallas_call | solution.py:54
  68.2 0.0 copy-start
  68.2 1.9 copy-done
  70.1 0.0 reduce-scatter.2.cloned.1.call-update
  70.1 0.0 all-reduce.2.cloned.1.call-start
  70.2 90.3 %reduce-scatter.2.cloned.1.call-done.refs_1_ = f32[64,512]{1,0:T(8,128)} async-done(((f32[2048,512]{1,0:T(8,128)}), f32[64,512]{1,0:T(8,128)}) %reduce-scatter.2.cloned.1.call-update) | async-done | bytes 131088 | tf_op jit(solution)/shard_map/reduce_scatter | solution.py:145
  160.4 3.0 fusion.1
  163.5 0.0 all-reduce.2.cloned.1.call-update
  163.5 258.8 %all-reduce.2.cloned.1.call-done.refs_0_ = f32[512,512]{1,0:T(8,128)} async-done(((f32[512,512]{1,0:T(8,128)}), f32[512,512]{1,0:T(8,128)}) %all-reduce.2.cloned.1.call-update) | async-done | bytes 1048592 | tf_op jit(solution)/shard_map/psum | solution.py:147
  422.3 0.0 copy-start.3
  422.3 0.9 copy-done.3
  423.2 0.0 copy-start.4
  423.2 1.2 copy-done.4
  424.4 23.5 %cholesky_basis.1 = f32[64,512]{1,0:T(8,128)} custom-call(f32[512,512]{1,0:T(8,128)S(1)} %copy-done.4, f32[64,512]{1,0:T(8,128)S(1)} %copy-done.3), custom_call_target="tpu_custom_call" | custom-call | tf_op jit(solution)/shard_map/cholesky_basis/pallas_call | solution.py:124
  (1 shorter events, 0.0 us)
Async XLA Ops:
  6.5 43.8 %all-gather.2.cloned.1.call-start = ((), (), s32[]{:S(2)}) async-start(), calls=%async_computation.1 | async-start | bytes 2359296 | tf_op jit(solution)/shard_map/all_gather | solution.py:143
  7.3 153.2 %reduce-scatter.2.cloned.1.call-start = ((), (), s32[]{:S(2)}) async-start(), calls=%async_computation.2 | async-start | bytes 4325376 | tf_op jit(solution)/shard_map/reduce_scatter | solution.py:145
  50.4 2.8 copy-start.1
  53.2 1.6 copy-start.2
  68.2 1.9 copy-start
  70.1 352.2 %all-reduce.2.cloned.1.call-start = ((), (), s32[]{:S(2)}) async-start(), calls=%async_computation.3 | async-start | bytes 2097152 | tf_op jit(solution)/shard_map/psum | solution.py:147
  422.3 0.9 copy-start.3
  423.2 1.2 copy-start.4
Sparse Core Ops, SparseCore 0:
  9.1 41.1 all-gather.1
  70.2 90.1 reduce-scatter.1
  166.8 255.4 all-reduce.1

commit v2 on v1

--- a/solution.py
+++ b/solution.py
@@ -14,6 +14,14 @@
 SLOTS = 48
 VMEM = pltpu.VMEM
 SMEM = pltpu.SMEM
+MESH = pl.DeviceIdType.MESH
+
+CHIPS = 16
+DEPTH = 8
+BLOCKS = [(i, j) for i in range(4) for j in range(i, 4)]
+WHERE = {ij: n * 128 for n, ij in enumerate(BLOCKS)}
+HALF = 640
+PIECE = 40
 
 
 def mm(a, b, dims):
@@ -99,37 +107,162 @@
             w_ref[e:, :] = w_ref[e:, :] - t[e:, :]
 
 
-def basis_kernel(scale, gram_ref, rows_ref, out_ref, s_ref, w_ref):
+def gram_kernel(scale, rows_ref, out_ref, mine, twin, parts, planes, gram, x_ref, s_ref, w_ref,
+                pair_send, pair_recv, part_send, part_recv, plane_send, plane_recv, gather_send, gather_recv):
+    row, z = lax.axis_index("row"), lax.axis_index("col")
+    chip, core = row // 2, row % 2
+    other = 1 - core
+
+    def at_chip(i):
+        return (lax.rem(chip + i, CHIPS) * 2 + core, z)
+
+    def at_plane(i):
+        return (row, lax.rem(z + i, DEPTH))
+
+    twin_id = (chip * 2 + other, z)
+    barrier = pltpu.get_barrier_semaphore()
+
+    def hello_chip(i, c):
+        pl.semaphore_signal(barrier, inc=1, device_id=at_chip(i), device_id_type=MESH)
+        return c
+
+    def hello_plane(i, c):
+        pl.semaphore_signal(barrier, inc=1, device_id=at_plane(i), device_id_type=MESH)
+        return c
+
+    pl.semaphore_signal(barrier, inc=1, device_id=twin_id, device_id_type=MESH)
+    lax.fori_loop(1, CHIPS, hello_chip, 0)
+    lax.fori_loop(1, DEPTH, hello_plane, 0)
+
+    for i in range(4):
+        g = mm(rows_ref[:, i * 128:(i + 1) * 128], rows_ref[:, i * 128:], ((0,), (0,)))
+        for j in range(i, 4):
+            at = WHERE[i, j]
+            mine[at:at + 128, :] = g[:, (j - i) * 128:(j - i + 1) * 128]
+    pl.semaphore_wait(barrier, 1 + CHIPS - 1 + DEPTH - 1)
+
+    copy = pltpu.make_async_remote_copy(
+        src_ref=mine.at[pl.ds(pl.multiple_of(other * HALF, 8), HALF)], dst_ref=twin,
+        send_sem=pair_send.at[0], recv_sem=pair_recv.at[0], device_id=twin_id, device_id_type=MESH)
+    copy.start()
+    copy.wait()
+    own = pl.ds(pl.multiple_of(core * HALF, 8), HALF)
+    twin[...] = twin[...] + mine[own, :]
+
+    def part(i):
+        there = lax.rem(chip + i, CHIPS)
+        return pltpu.make_async_remote_copy(
+            src_ref=twin.at[pl.ds(pl.multiple_of(there * PIECE, 8), PIECE)], dst_ref=parts.at[i],
+            send_sem=part_send.at[i], recv_sem=part_recv.at[i], device_id=at_chip(i), device_id_type=MESH)
+
+    def start_part(i, c):
+        part(i).start()
+        return c
+
+    lax.fori_loop(1, CHIPS, start_part, 0)
+
+    def add_part(i, total):
+        part(i).wait()
+        return total + parts[i]
+
+    total = lax.fori_loop(1, CHIPS, add_part, twin[pl.ds(pl.multiple_of(chip * PIECE, 8), PIECE), :])
+
+    planes[z] = total
+
+    def plane(i):
+        return pltpu.make_async_remote_copy(
+            src_ref=planes.at[z], dst_ref=planes.at[z],
+            send_sem=plane_send.at[i], recv_sem=plane_recv.at[i], device_id=at_plane(i), device_id_type=MESH)
+
+    def start_plane(i, c):
+        plane(i).start()
+        return c
+
+    def wait_plane(i, c):
+        plane(i).wait_send()
+        came = lax.rem(z + DEPTH - i, DEPTH)
+        pltpu.make_async_remote_copy(
+            src_ref=planes.at[came], dst_ref=planes.at[came],
+            send_sem=plane_send.at[i], recv_sem=plane_recv.at[i], device_id=at_plane(i), device_id_type=MESH).wait_recv()
+        return c
+
+    lax.fori_loop(1, DEPTH, start_plane, 0)
+    lax.fori_loop(1, DEPTH, wait_plane, 0)
+    total = planes[0]
+    for i in range(1, DEPTH):
+        total = total + planes[i]
+
+    def slot(n):
+        return pl.ds(pl.multiple_of(core * HALF + n * PIECE, 8), PIECE)
+
+    gram[slot(chip), :] = total
+
+    def start_gather(i, c):
+        pltpu.make_async_remote_copy(
+            src_ref=gram.at[slot(chip)], dst_ref=gram.at[slot(chip)],
+            send_sem=gather_send.at[i], recv_sem=gather_recv.at[i], device_id=at_chip(i), device_id_type=MESH).start()
+        return c
+
+    def wait_gather(i, c):
+        came = lax.rem(chip + CHIPS - i, CHIPS)
+        pltpu.make_async_remote_copy(
+            src_ref=gram.at[slot(came)], dst_ref=gram.at[slot(came)],
+            send_sem=gather_send.at[i], recv_sem=gather_recv.at[i], device_id=at_chip(i), device_id_type=MESH).wait()
+        return c
+
+    lax.fori_loop(1, CHIPS, start_gather, 0)
+    lax.fori_loop(1, CHIPS, wait_gather, 0)
+    there = pl.ds(pl.multiple_of(other * HALF, 8), HALF)
+    copy = pltpu.make_async_remote_copy(
+        src_ref=gram.at[own], dst_ref=gram.at[own],
+        send_sem=pair_send.at[1], recv_sem=pair_recv.at[1], device_id=twin_id, device_id_type=MESH)
+    copy.start()
+    copy.wait_send()
+    pltpu.make_async_remote_copy(
+        src_ref=gram.at[there], dst_ref=gram.at[there],
+        send_sem=pair_send.at[1], recv_sem=pair_recv.at[1], device_id=twin_id, device_id_type=MESH).wait_recv()
+
     eye = (
         lax.broadcasted_iota(jnp.int32, (128, 128), 0)
         == lax.broadcasted_iota(jnp.int32, (128, 128), 1)
     ).astype(F32)
-    s_ref[...] = gram_ref[...]
-    out_ref[...] = rows_ref[...]
-    for i in range(K // 128):
+    for i, j in BLOCKS:
+        at = WHERE[i, j]
+        s_ref[i * 128:(i + 1) * 128, j * 128:(j + 1) * 128] = gram[at:at + 128, :]
+    x_ref[...] = rows_ref[...]
+    for i in range(4):
         lo, hi = i * 128, (i + 1) * 128
         w_ref[:, :128] = s_ref[lo:hi, lo:hi]
         w_ref[:, 128:] = eye
         factor(w_ref, 16)
         inv = w_ref[:, 128:]
-        x = mm(out_ref[:, lo:hi], inv, ((1,), (1,)))
+        x = mm(x_ref[:, lo:hi], inv, ((1,), (1,)))
         out_ref[:, lo:hi] = x * scale
         if hi < K:
             u = mm(inv, s_ref[lo:hi, hi:], ((1,), (0,)))
-            s_ref[hi:, hi:] = s_ref[hi:, hi:] - mm(u, u, ((0,), (0,)))
-            out_ref[:, hi:] = out_ref[:, hi:] - mm(x, u, ((1,), (0,)))
-
-
-def cholesky_basis(gram, rows, scale):
+            for j in range(i + 1, 4):
+                a, b = j * 128, (j + 1) * 128
+                s_ref[a:b, a:] = s_ref[a:b, a:] - mm(u[:, a - hi:b - hi], u[:, a - hi:], ((0,), (0,)))
+            x_ref[:, hi:] = x_ref[:, hi:] - mm(x, u, ((1,), (0,)))
+
+
+def gram_basis(rows, scale):
+    dma = pltpu.SemaphoreType.DMA
     return pl.pallas_call(
-        lambda *refs: basis_kernel(scale, *refs),
+        lambda *refs: gram_kernel(scale, *refs),
         out_shape=jax.ShapeDtypeStruct(rows.shape, F32),
-        in_specs=[pl.BlockSpec(memory_space=VMEM)] * 2,
+        in_specs=[pl.BlockSpec(memory_space=VMEM)],
         out_specs=pl.BlockSpec(memory_space=VMEM),
-        scratch_shapes=[VMEM((K, K), F32), VMEM((128, 256), F32)],
-        compiler_params=pltpu.CompilerParams(vmem_limit_bytes=40 * 2**20),
-        name="cholesky_basis",
-    )(gram, rows)
+        scratch_shapes=[
+            VMEM((2 * HALF, 128), F32), VMEM((HALF, 128), F32), VMEM((CHIPS, PIECE, 128), F32),
+            VMEM((DEPTH, PIECE, 128), F32), VMEM((2 * HALF, 128), F32), VMEM((64, K), F32),
+            VMEM((K, K), F32), VMEM((128, 256), F32),
+            dma((2,)), dma((2,)), dma((CHIPS,)), dma((CHIPS,)), dma((DEPTH,)), dma((DEPTH,)), dma((CHIPS,)), dma((CHIPS,)),
+        ],
+        compiler_params=pltpu.CompilerParams(
+            vmem_limit_bytes=40 * 2**20, collective_id=1, has_side_effects=True),
+        name="gram_basis",
+    )(rows)
 
 
 def local(tiles, coords, counts, panel):
@@ -143,10 +276,8 @@
     gathered = lax.all_gather(panel, "col", axis=0, tiled=True)
     partial_sum = tile_product(slot_of, tiles[0, 0], gathered)
     own_rows = lax.psum_scatter(partial_sum, "row", scatter_dimension=0, tiled=True)
-    local_gram = mm(own_rows, own_rows, ((0,), (0,)))
-    gram = lax.psum(local_gram, ("row", "col"))
     scale = float((partial_sum.shape[0] * 8) ** 0.5)
-    return cholesky_basis(gram, own_rows, scale)
+    return gram_basis(own_rows, scale)
 
 
 def solution(mesh):

time: 455 us -> 223 us (0.49)
  waiting for transfers between devices: 391 us -> 133 us
  Pallas kernels: 36.9 us -> 67.8 us
    psum x1 -> x0, waiting for transfers between devices: 259 us -> none  [local(): gram = lax.psum(local_gram, ('row', 'col'))]
    pallas_call x1, Pallas kernels: 23.5 us -> 54.4 us  [gram_basis(): pl.pallas_call(lambda *refs: gram_kernel(scale, *refs), out_shape=jax.Sha...]
  transfers between devices with their start and end apart: 3 -> 2, of which waited for: 3 -> 2; matrix products, arithmetic and copies ran while one was open for 0% -> 0% of each run, Pallas kernels for 0% -> 0%
where the time goes in v2:
time: 223 us
  waiting for transfers between devices  133 us (60%)
  Pallas kernels  67.8 us (30%)
  between operations  14.1 us (6%)
  local copies, waits for them, and re-layouts  7.87 us (4%)
    reduce_scatter x1, waiting for transfers between devices, local(): lax.psum_scatter(partial_sum, 'row', scatter_dimension=0, tiled=True)  90.3 us
    pallas_call x1, Pallas kernels, gram_basis(): pl.pallas_call(lambda *refs: gram_kernel(scale, *refs), out_shape=jax.Sha...  54.4 us
    all_gather x1, waiting for transfers between devices, local(): gathered = lax.all_gather(panel, 'col', axis=0, tiled=True)  41.6 us
    pallas_call x1, Pallas kernels, tile_product(): pl.pallas_call(tile_kernel, out_shape=jax.ShapeDtypeStruct((NB * TILE, K)...  13.4 us
    unnamed x9, local copies, waits for them, and re-layouts  7.87 us
  transfers between devices with their start and end apart: 2, of which 2 were waited for; matrix products, arithmetic and copies ran while one was open for 0% of the time, Pallas kernels for 0%

profile of v2, /device:TPU:1, one launch (start us, length us, event | category | flops | bytes accessed | tf_op | source)
XLA Modules:
  0.0 223.3 jit_solution(18158403034642850735)
XLA Ops:
  6.5 0.0 all-gather.2.cloned.1.call-start
  6.5 0.7 all-gather.2.cloned.1.call-update
  7.3 0.0 reduce-scatter.2.cloned.1.call-start
  8.0 0.8 add_bitcast_fusion
  8.7 0.1 select_reduce_fusion.slot_ref
  8.8 41.6 %all-gather.2.cloned.1.call-done.panel_ref = bf16[2048,512]{1,0:T(8,128)(2,1)} async-done(((bf16[256,512]{1,0:T(8,128)(2,1)}), bf16[2048,512]{1,0:T(8,128)(2,1)}) %all-gather.2.cloned.1.call-update) | async-done | bytes 2097168 | tf_op jit(solution)/shard_map/all_gather | solution.py:276
  50.4 0.0 copy-start.1
  50.4 2.8 %copy-done.1 = bf16[1,1,48,256,256]{4,3,2,1,0:T(8,128)(2,1)S(1)} copy-done((bf16[1,1,48,256,256]{4,3,2,1,0:T(8,128)(2,1)S(1)}, bf16[1,1,48,256,256]{4,3,2,1,0:T(8,128)(2,1)}, u32[]{:S(2)}) %copy-start.1) | copy-done | bytes 6291480
  53.2 0.0 copy-start.2
  53.2 1.6 copy-done.2
  54.8 13.4 %tile_product.1 = f32[2048,512]{1,0:T(8,128)S(1)} custom-call(s32[64]{0:T(128)S(1)} %select_reduce_fusion.slot_ref, bf16[48,256,256]{2,1,0:T(8,128)(2,1)S(1)} %bitcast.6, bf16[2048,512]{1,0:T(8,128)(2,1)S(1)} %copy-done.2), custom_call_target="tpu_custom_call" | custom-call | tf_op jit(solution)/shard_map/tile_product/pallas_call | solution.py:62
  68.2 0.0 copy-start
  68.2 1.9 copy-done
  70.1 0.0 reduce-scatter.2.cloned.1.call-update
  70.1 90.3 %reduce-scatter.2.cloned.1.call-done.refs_0_ = f32[64,512]{1,0:T(8,128)} async-done(((f32[2048,512]{1,0:T(8,128)}), f32[64,512]{1,0:T(8,128)}) %reduce-scatter.2.cloned.1.call-update) | async-done | bytes 131088 | tf_op jit(solution)/shard_map/reduce_scatter | solution.py:278
  160.5 0.0 copy-start.3
  160.5 0.9 copy-done.3
  161.4 54.4 %gram_basis.1 = f32[64,512]{1,0:T(8,128)S(1)} custom-call(f32[64,512]{1,0:T(8,128)S(1)} %copy-done.3), custom_call_target="tpu_custom_call" | custom-call | tf_op jit(solution)/shard_map/gram_basis/pallas_call | solution.py:251
  215.8 0.7 copy.7
  (1 shorter events, 0.0 us)
Async XLA Ops:
  6.5 43.8 %all-gather.2.cloned.1.call-start = ((), (), s32[]{:S(2)}) async-start(), calls=%async_computation.1 | async-start | bytes 2359296 | tf_op jit(solution)/shard_map/all_gather | solution.py:276
  7.3 153.2 %reduce-scatter.2.cloned.1.call-start = ((), (), s32[]{:S(2)}) async-start(), calls=%async_computation.2 | async-start | bytes 4325376 | tf_op jit(solution)/shard_map/reduce_scatter | solution.py:278
  50.4 2.8 %copy-start.1 = (bf16[1,1,48,256,256]{4,3,2,1,0:T(8,128)(2,1)S(1)}, bf16[1,1,48,256,256]{4,3,2,1,0:T(8,128)(2,1)}, u32[]{:S(2)}) copy-start(bf16[1,1,48,256,256]{4,3,2,1,0:T(8,128)(2,1)} %param.4) | copy-start | bytes 18874372
  53.2 1.6 copy-start.2
  68.2 1.9 copy-start
  160.5 0.9 copy-start.3
Sparse Core Ops, SparseCore 0:
  9.1 41.1 all-gather.1
  70.2 90.1 reduce-scatter.1

commit v3 on v2

--- a/solution.py
+++ b/solution.py
@@ -18,6 +18,8 @@
 
 CHIPS = 16
 DEPTH = 8
+NQ = 4
+W = 128
 BLOCKS = [(i, j) for i in range(4) for j in range(i, 4)]
 WHERE = {ij: n * 128 for n, ij in enumerate(BLOCKS)}
 HALF = 640
@@ -26,56 +28,6 @@
 
 def mm(a, b, dims):
     return lax.dot_general(a, b, (dims, ((), ())), precision=HI, preferred_element_type=F32)
-
-
-def tile_kernel(slot_ref, tiles_hbm, panel_ref, out_ref, tiles_ref, at_ref, sem):
-    copy = pltpu.make_async_copy(tiles_hbm, tiles_ref, sem)
-    copy.start()
-    copy.wait()
-
-    def build(pos, carry):
-        slot = slot_ref[pos]
-        tile = tiles_ref[jnp.minimum(slot, SLOTS - 1)]
-        tile = jnp.where(slot < SLOTS, tile.astype(F32), 0.0).T.astype(BF16)
-        block_row, block_col = pos // NB, pos % NB
-        at_ref[block_row, pl.ds(pl.multiple_of(block_col * TILE, TILE), TILE), :] = tile
-        return carry
-
-    lax.fori_loop(0, NB * NB, build, 0)
-
-    def multiply(col, carry):
-        rows = pl.ds(pl.multiple_of(col * TILE, TILE), TILE)
-        total = jnp.zeros((TILE, K), F32)
-        for b in range(NB):
-            total += jnp.dot(
-                at_ref[b, rows, :],
-                panel_ref[b * TILE:(b + 1) * TILE, :],
-                preferred_element_type=F32,
-            )
-        out_ref[rows, :] = total
-        return carry
-
-    lax.fori_loop(0, NB, multiply, 0)
-
-
-def tile_product(slot_of, tiles, panel):
-    return pl.pallas_call(
-        tile_kernel,
-        out_shape=jax.ShapeDtypeStruct((NB * TILE, K), F32),
-        in_specs=[
-            pl.BlockSpec(memory_space=SMEM),
-            pl.BlockSpec(memory_space=pl.ANY),
-            pl.BlockSpec(memory_space=VMEM),
-        ],
-        out_specs=pl.BlockSpec(memory_space=VMEM),
-        scratch_shapes=[
-            VMEM((SLOTS, TILE, TILE), BF16),
-            VMEM((NB, NB * TILE, TILE), BF16),
-            pltpu.SemaphoreType.DMA,
-        ],
-        compiler_params=pltpu.CompilerParams(vmem_limit_bytes=40 * 2**20),
-        name="tile_product",
-    )(slot_of, tiles, panel)
 
 
 def factor(w_ref, b):
@@ -265,6 +217,221 @@
     )(rows)
 
 
+def product_kernel(slot_ref, tiles_hbm, panel_ref, out_ref, tiles_ref, at_ref, pan, part, twin, near, far, final, last,
+                   tile_sem, ring_send, ring_recv, pair_send, pair_recv, near_send, near_recv,
+                   far_send, far_recv, last_send, last_recv):
+    row, z = lax.axis_index("row"), lax.axis_index("col")
+    core, x, y = row % 2, (row // 2) % 4, row // 8
+    other = 1 - core
+
+    def device(yy, xx, cc, zz):
+        return ((yy * 4 + xx) * 2 + cc, zz)
+
+    def ring4(v, step):
+        return lax.rem(v + step + 4, 4)
+
+    up = device(y, x, core, lax.rem(z + 1, DEPTH))
+    down = device(y, x, core, lax.rem(z + DEPTH - 1, DEPTH))
+    twin_id = device(y, x, other, z)
+
+    def along(axis, step):
+        return device(y, ring4(x, step), core, z) if axis == 0 else device(ring4(y, step), x, core, z)
+
+    barrier = pltpu.get_barrier_semaphore()
+    peers = [up, down, twin_id] + [along(a, s) for a in (0, 1) for s in (1, 2, 3)]
+    for peer in peers:
+        pl.semaphore_signal(barrier, inc=1, device_id=peer, device_id_type=MESH)
+    fetch = pltpu.make_async_copy(tiles_hbm, tiles_ref, tile_sem)
+    fetch.start()
+    for q in range(NQ):
+        pan[q, z] = panel_ref[:, q * W:(q + 1) * W]
+    pl.semaphore_wait(barrier, len(peers))
+
+    def remote(src, dst, send, recv, peer):
+        return pltpu.make_async_remote_copy(
+            src_ref=src, dst_ref=dst, send_sem=send, recv_sem=recv, device_id=peer, device_id_type=MESH)
+
+    def hop(q, h, way):
+        block = lax.rem(z - h + DEPTH, DEPTH) if way == 0 else lax.rem(z + h, DEPTH)
+        ref = pan.at[q, block]
+        if h == 3:
+            ref = ref.at[pl.ds(0, TILE // 2)] if way == 0 else ref.at[pl.ds(TILE // 2, TILE // 2)]
+        return remote(ref, ref, ring_send.at[way, q, h], ring_recv.at[way, q, h], up if way == 0 else down)
+
+    def came(q, h, way):
+        block = lax.rem(z - 1 - h + DEPTH, DEPTH) if way == 0 else lax.rem(z + 1 + h, DEPTH)
+        ref = pan.at[q, block]
+        if h == 3:
+            ref = ref.at[pl.ds(0, TILE // 2)] if way == 0 else ref.at[pl.ds(TILE // 2, TILE // 2)]
+        remote(ref, ref, ring_send.at[way, q, h], ring_recv.at[way, q, h], up if way == 0 else down).wait_recv()
+
+    def slot(s):
+        q, h = 2 * (s // 8) + s % 2, (s % 8) // 2
+        for way in (0, 1):
+            if h > 0:
+                came(q, h - 1, way)
+            hop(q, h, way).start()
+
+    def build(b):
+        def one(i, carry):
+            n = slot_ref[b * NB + i]
+            tile = tiles_ref[jnp.minimum(n, SLOTS - 1)]
+            tile = jnp.where(n < SLOTS, tile, jnp.zeros_like(tile)).T
+            for xl in range(2):
+                for c in range(2):
+                    at = (xl * 2 + c) * 64
+                    to = pl.multiple_of((2 * (i % 2) + xl) * 64, 64)
+                    at_ref[b, c, i // 2, pl.ds(to, 64), :] = tile[at:at + 64, :]
+            return carry
+
+        lax.fori_loop(0, NB, one, 0)
+
+    def multiply(q, c):
+        def one(m, carry):
+            total = jnp.dot(at_ref[0, c, m], pan[q, 0], preferred_element_type=F32)
+            for b in range(1, NB):
+                total += jnp.dot(at_ref[b, c, m], pan[q, b], preferred_element_type=F32)
+            for xx in range(4):
+                piece = total[xx * 64:(xx + 1) * 64, :]
+                if q % 2 == 0:
+                    part[q, c, xx, m] = piece
+                else:
+                    part[q, c, m, xx] = piece
+            return carry
+
+        lax.fori_loop(0, 4, one, 0)
+
+    def to_twin(q):
+        return remote(part.at[q, other], twin.at[q], pair_send.at[q], pair_recv.at[q], twin_id)
+
+    def compute(q):
+        came(q, 3, 0)
+        came(q, 3, 1)
+        multiply(q, other)
+        to_twin(q).start()
+        multiply(q, core)
+
+    def here(q):
+        return x if q % 2 == 0 else y
+
+    def near_copy(q, n):
+        step, half = ((2, 0), (1, 2), (2, 2), (-1, 0))[n]
+        ref = twin.at[q, ring4(here(q), step), pl.ds(half, 2)]
+        return remote(ref, near.at[q, n], near_send.at[q, n], near_recv.at[q, n], along(q % 2, 1 if n < 2 else -1))
+
+    def far_copy(q, n):
+        return remote(near.at[q, 2 * n], far.at[q, n], far_send.at[q, n], far_recv.at[q, n], along(q % 2, 1 - 2 * n))
+
+    def stage1(q):
+        to_twin(q).wait_recv()
+        twin[q] = twin[q] + part[q, core]
+        for n in range(4):
+            near_copy(q, n).start()
+
+    def stage2(q):
+        u = here(q)
+        near_copy(q, 0).wait_recv()
+        near[q, 0] = near[q, 0] + twin[q, ring4(u, 1), 0:2]
+        far_copy(q, 0).start()
+        near_copy(q, 2).wait_recv()
+        near[q, 2] = near[q, 2] + twin[q, ring4(u, -1), 2:4]
+        far_copy(q, 1).start()
+
+    def last_copy(q, s):
+        return remote(final.at[q, ring4(here(q + 1), s)], last.at[q, s], last_send.at[q, s], last_recv.at[q, s], along(1 - q % 2, s))
+
+    def stage3(q):
+        u = here(q)
+        near_copy(q, 1).wait_recv()
+        near_copy(q, 3).wait_recv()
+        far_copy(q, 0).wait_recv()
+        final[q, 0:2] = twin[q, u, 0:2] + near[q, 3] + far[q, 0]
+        far_copy(q, 1).wait_recv()
+        final[q, 2:4] = twin[q, u, 2:4] + near[q, 1] + far[q, 1]
+        for s in (1, 2, 3):
+            last_copy(q, s).start()
+
+    def stage4(q):
+        v = here(q + 1)
+        for s in (1, 2, 3):
+            last_copy(q, s).wait_recv()
+        out_ref[:, q * W:(q + 1) * W] = final[q, v] + last[q, 1] + last[q, 2] + last[q, 3]
+
+    slot(0)
+    slot(1)
+    fetch.wait()
+    build(0)
+    for s in range(2, 8):
+        slot(s)
+        build(s - 1)
+    build(7)
+    slot(8)
+    slot(9)
+    compute(0)
+    slot(10)
+    compute(1)
+    slot(11)
+    stage1(0)
+    slot(12)
+    stage1(1)
+    slot(13)
+    stage2(0)
+    slot(14)
+    stage2(1)
+    slot(15)
+    stage3(0)
+    stage3(1)
+    compute(2)
+    compute(3)
+    stage4(0)
+    stage4(1)
+    for stage in (stage1, stage2, stage3, stage4):
+        stage(2)
+        stage(3)
+
+    for q in range(NQ):
+        for h in range(4):
+            for way in (0, 1):
+                hop(q, h, way).wait_send()
+        to_twin(q).wait_send()
+        for n in range(4):
+            near_copy(q, n).wait_send()
+        for n in range(2):
+            far_copy(q, n).wait_send()
+        for s in (1, 2, 3):
+            last_copy(q, s).wait_send()
+
+
+def product_rows(slot_of, tiles, panel):
+    dma = pltpu.SemaphoreType.DMA
+    return pl.pallas_call(
+        product_kernel,
+        out_shape=jax.ShapeDtypeStruct((64, K), F32),
+        in_specs=[
+            pl.BlockSpec(memory_space=SMEM),
+            pl.BlockSpec(memory_space=pl.ANY),
+            pl.BlockSpec(memory_space=VMEM),
+        ],
+        out_specs=pl.BlockSpec(memory_space=VMEM),
+        scratch_shapes=[
+            VMEM((SLOTS, TILE, TILE), BF16),
+            VMEM((NB, 2, 4, TILE, TILE), BF16),
+            VMEM((NQ, DEPTH, TILE, W), BF16),
+            VMEM((NQ, 2, 4, 4, 64, W), F32),
+            VMEM((NQ, 4, 4, 64, W), F32),
+            VMEM((NQ, 4, 2, 64, W), F32),
+            VMEM((NQ, 2, 2, 64, W), F32),
+            VMEM((NQ, 4, 64, W), F32),
+            VMEM((NQ, 4, 64, W), F32),
+            dma, dma((2, NQ, 4)), dma((2, NQ, 4)), dma((NQ,)), dma((NQ,)), dma((NQ, 4)), dma((NQ, 4)),
+            dma((NQ, 2)), dma((NQ, 2)), dma((NQ, 4)), dma((NQ, 4)),
+        ],
+        compiler_params=pltpu.CompilerParams(
+            vmem_limit_bytes=56 * 2**20, collective_id=0, has_side_effects=True),
+        name="product_rows",
+    )(slot_of, tiles, panel)
+
+
 def local(tiles, coords, counts, panel):
     where = coords[0, 0]
     position = where[:, 0] * NB + where[:, 1]
@@ -273,10 +440,8 @@
     match = (position[None, :] == jnp.arange(NB * NB, dtype=jnp.int32)[:, None]) & live[None, :]
     slot_of = jnp.min(jnp.where(match, slots[None, :], SLOTS), axis=1)
 
-    gathered = lax.all_gather(panel, "col", axis=0, tiled=True)
-    partial_sum = tile_product(slot_of, tiles[0, 0], gathered)
-    own_rows = lax.psum_scatter(partial_sum, "row", scatter_dimension=0, tiled=True)
-    scale = float((partial_sum.shape[0] * 8) ** 0.5)
+    own_rows = product_rows(slot_of, tiles[0, 0], panel)
+    scale = float((NB * TILE * DEPTH) ** 0.5)
     return gram_basis(own_rows, scale)
 
 

time: 223 us -> 116 us (0.52)
  waiting for transfers between devices: 133 us -> 0 us
  Pallas kernels: 67.8 us -> 112 us
  between operations: 14.1 us -> 0.68 us
  local copies, waits for them, and re-layouts: 7.87 us -> 1.56 us
    reduce_scatter x1 -> x0, waiting for transfers between devices: 90.3 us -> none  [local(): lax.psum_scatter(partial_sum, 'row', scatter_dimension=0, tiled=True)]
    pallas_call x1, Pallas kernels: 13.4 us -> 60.4 us  [product_rows(): pl.pallas_call(product_kernel, out_shape=jax.ShapeDtypeStruct((64, K), F3...]
    all_gather x1 -> x0, waiting for transfers between devices: 41.6 us -> none  [local(): gathered = lax.all_gather(panel, 'col', axis=0, tiled=True)]
    unnamed x9 -> x3, local copies, waits for them, and re-layouts: 7.87 us -> 1.56 us
    pallas_call x1, Pallas kernels: 54.4 us -> 51.5 us  [gram_basis(): pl.pallas_call(lambda *refs: gram_kernel(scale, *refs), out_shape=jax.Sha...]
  transfers between devices with their start and end apart: 2 -> 0, of which waited for: 2 -> 0; matrix products, arithmetic and copies ran while one was open for 0% -> 0% of each run, Pallas kernels for 0% -> 0%
where the time goes in v3:
time: 116 us
  Pallas kernels  112 us (97%)
  local copies, waits for them, and re-layouts  1.56 us (1%)
  other arithmetic  1.38 us (1%)
    pallas_call x1, Pallas kernels, product_rows(): pl.pallas_call(product_kernel, out_shape=jax.ShapeDtypeStruct((64, K), F3...  60.4 us
    pallas_call x1, Pallas kernels, gram_basis(): pl.pallas_call(lambda *refs: gram_kernel(scale, *refs), out_shape=jax.Sha...  51.5 us

profile of v3, /device:TPU:1, one launch (start us, length us, event | category | flops | bytes accessed | tf_op | source)
XLA Modules:
  0.0 115.5 jit_solution(885707262813408893)
XLA Ops:
  0.7 0.8 add_bitcast_fusion
  1.4 0.6 select_reduce_fusion.slot_ref
  2.0 60.4 %product_rows.1.refs_0_ = f32[64,512]{1,0:T(8,128)} custom-call(s32[64]{0:T(128)} %select_reduce_fusion.slot_ref, bf16[48,256,256]{2,1,0:T(8,128)(2,1)} %bitcast.6, bf16[256,512]{1,0:T(8,128)(2,1)} %panel_ref.1), custom_call_target="tpu_custom_call" | custom-call | tf_op jit(solution)/shard_map/product_rows/pallas_call | solution.py:407
  62.5 0.0 copy-start
  62.5 0.9 copy-done
  63.4 51.5 %gram_basis.1 = f32[64,512]{1,0:T(8,128)S(1)} custom-call(f32[64,512]{1,0:T(8,128)S(1)} %copy-done), custom_call_target="tpu_custom_call" | custom-call | tf_op jit(solution)/shard_map/gram_basis/pallas_call | solution.py:203
  114.8 0.7 copy.7
  (1 shorter events, 0.0 us)
Async XLA Ops:
  62.5 0.9 copy-start

commit v4 on v0

v4 whole, which is shorter than its diff:
```python
import jax
import jax.numpy as jnp
from jax import lax
from jax.experimental import pallas as pl
from jax.experimental.pallas import tpu as pltpu
from jax.sharding import PartitionSpec as P

F32 = jnp.float32
BF16 = jnp.bfloat16
HI = lax.Precision.HIGHEST
MESH = pl.DeviceIdType.MESH
VMEM = pltpu.VMEM
SMEM = pltpu.SMEM
TILE = 256
NB = 8
K = 512
SLOTS = 48
CHIPS = 16
DEPTH = 8
W = 128
NQ = 4
OWN = 64
PANEL = 16


def mm(a, b, dims):
    return lax.dot_general(a, b, (dims, ((), ())), precision=HI, preferred_element_type=F32)


def split(v):
    hi = v.astype(BF16)
    rest = v - hi.astype(F32)
    mid = rest.astype(BF16)
    return hi, mid, (rest - mid.astype(F32)).astype(BF16)


def stacked(a, b):
    ah, am, al = split(a)
    bh, bm, bl = split(b)
    return lax.dot_general(
        jnp.concatenate([ah, ah, am, am, ah, al], axis=0),
        jnp.concatenate([bh, bm, bh, bm, bl, bh], axis=0),
        (((0,), (0,)), ((), ())),
        preferred_element_type=F32,
    )


def factor(w):
    sub = lax.broadcasted_iota(jnp.int32, (PANEL, W), 0)
    rows = [w[c:c + PANEL, :] for c in range(0, W, PANEL)]
    for k in range(W // PANEL):
        c0 = k * PANEL
        left, right = rows[k][:, :W], rows[k][:, W:]
        cols = [jnp.broadcast_to(left[:, c0 + j:c0 + j + 1], (PANEL, W)) for j in range(PANEL)]
        pivots = jnp.ones((PANEL, W), F32)
        for j in range(PANEL):
            pivot = cols[j][j:j + 1, :]
            f = jnp.where(sub > j, cols[j] * (1.0 / pivot), 0.0)
            for m in range(j + 1, PANEL):
                cols[m] = cols[m] - f * cols[m][j:j + 1, :]
            if j < PANEL - 1:
                left = left - f * left[j:j + 1, :]
                right = right - f * right[j:j + 1, :]
            pivots = jnp.where(sub == j, pivot, pivots)
        norm = lax.rsqrt(pivots)
        left = left * norm
        rows[k] = jnp.concatenate([left, right * norm], axis=1)
        if c0 + PANEL < W:
            t = stacked(left, rows[k])
            for m in range(k + 1, W // PANEL):
                rows[m] = rows[m] - t[m * PANEL:(m + 1) * PANEL, :]
        yield
    return jnp.concatenate(rows, axis=0)


def fused_kernel(scale, slot_ref, tiles_hbm, panel_ref, out_ref, tiles_ref, at_ref, pan, part, twin, near, far, final,
                 last, x_ref, s_ref, u_ref, *rest):
    bufs = (rest[0:5], rest[5:10])
    (tile_sem, ring_send, ring_recv, pair_send, pair_recv, near_send, near_recv, far_send, far_recv,
     last_send, last_recv) = rest[10:21]
    sems = (rest[21:29], rest[29:37])
    row, z = lax.axis_index("row"), lax.axis_index("col")
    core, chip = row % 2, row // 2
    x, y = chip % 4, chip // 4
    other = 1 - core

    def device(yy, xx, cc, zz):
        return ((yy * 4 + xx) * 2 + cc, zz)

    def ring4(v, step):
        return lax.rem(v + step + 4, 4)

    def at_chip(i):
        return (lax.rem(chip + i, CHIPS) * 2 + core, z)

    def at_plane(i):
        return (row, lax.rem(z + i, DEPTH))

    up, down = at_plane(1), at_plane(DEPTH - 1)
    twin_id = device(y, x, other, z)

    def along(axis, step):
        return device(y, ring4(x, step), core, z) if axis == 0 else device(ring4(y, step), x, core, z)

    def hello(device_of):
        def one(i, carry):
            pl.semaphore_signal(barrier, inc=1, device_id=device_of(i), device_id_type=MESH)
            return carry
        return one

    barrier = pltpu.get_barrier_semaphore()
    lax.fori_loop(1, DEPTH, hello(at_plane), 0)
    lax.fori_loop(1, CHIPS, hello(at_chip), 0)
    pl.semaphore_signal(barrier, inc=1, device_id=twin_id, device_id_type=MESH)
    fetch = pltpu.make_async_copy(tiles_hbm, tiles_ref, tile_sem)
    fetch.start()
    for p in range(2):
        pan[p, z] = panel_ref[:, p * TILE:(p + 1) * TILE]
    pl.semaphore_wait(barrier, DEPTH - 1 + CHIPS - 1 + 1)

    def remote(src, dst, send, recv, peer):
        return pltpu.make_async_remote_copy(
            src_ref=src, dst_ref=dst, send_sem=send, recv_sem=recv, device_id=peer, device_id_type=MESH)

    def ring_copy(p, a, h, way, block):
        ref = pan.at[p, block, pl.ds(a * 64, 64)]
        return remote(ref, ref, ring_send.at[way, p, a, h], ring_recv.at[way, p, a, h], up if way == 0 else down)

    def hop(p, a, h, way):
        return ring_copy(p, a, h, way, lax.rem(z + (DEPTH - h if way == 0 else h), DEPTH))

    def came(p, a, h, way):
        ring_copy(p, a, h, way, lax.rem(z + (DEPTH - 1 - h if way == 0 else 1 + h), DEPTH)).wait_recv()

    def ring(p, a, h):
        for way in (0, 1):
            piece = a + 2 if h == 3 and way == 1 else a
            if h > 0:
                came(p, piece, h - 1, way)
            hop(p, piece, h, way).start()

    def finish(p):
        for a in (0, 1):
            came(p, a + 2, 2, 0)
            came(p, a, 2, 1)
            came(p, a, 3, 0)
            came(p, a + 2, 3, 1)

    def build(part_of):
        b, first = part_of // 2, part_of % 2 * 4

        def one(i, carry):
            n = slot_ref[b * NB + i]
            tile = tiles_ref[jnp.minimum(n, SLOTS - 1)]
            tile = jnp.where(n < SLOTS, tile, jnp.zeros_like(tile)).T
            for xl in range(2):
                for c in range(2):
                    at = (xl * 2 + c) * 64
                    to = pl.multiple_of((2 * (i % 2) + xl) * 64, 64)
                    at_ref[b, c, i // 2, pl.ds(to, 64), :] = tile[at:at + 64, :]
            return carry

        lax.fori_loop(first, first + 4, one, 0)

    def pair_copy(q, m):
        if q % 2 == 0:
            src, dst = part.at[q, other, :, m], twin.at[q, :, m]
        else:
            src, dst = part.at[q, other, m], twin.at[q, m]
        return remote(src, dst, pair_send.at[q, m], pair_recv.at[q, m], twin_id)

    def multiply(p, c, m):
        total = jnp.dot(at_ref[0, c, m], pan[p, 0], preferred_element_type=F32)
        for b in range(1, NB):
            total += jnp.dot(at_ref[b, c, m], pan[p, b], preferred_element_type=F32)
        for xx in range(4):
            piece = total[xx * 64:(xx + 1) * 64, :]
            part[2 * p, c, xx, m] = piece[:, :W]
            part[2 * p + 1, c, m, xx] = piece[:, W:]

    def compute_other(p):
        def one(m, carry):
            multiply(p, other, m)
            pair_copy(2 * p, m).start()
            pair_copy(2 * p + 1, m).start()
            return carry
        lax.fori_loop(0, 4, one, 0)

    def compute_own(p):
        def one(m, carry):
            multiply(p, core, m)
            return carry
        lax.fori_loop(0, 4, one, 0)

    def here(q):
        return x if q % 2 == 0 else y

    def near_copy(q, n):
        step, half = ((2, 0), (1, 2), (2, 2), (-1, 0))[n]
        ref = twin.at[q, ring4(here(q), step), pl.ds(half, 2)]
        return remote(ref, near.at[q, n], near_send.at[q, n], near_recv.at[q, n], along(q % 2, 1 if n < 2 else -1))

    def far_copy(q, n):
        return remote(near.at[q, 2 * n], far.at[q, n], far_send.at[q, n], far_recv.at[q, n], along(q % 2, 1 - 2 * n))

    def last_copy(q, s):
        return remote(final.at[q, ring4(here(q + 1), s)], last.at[q, s], last_send.at[q, s], last_recv.at[q, s],
                      along(1 - q % 2, s))

    def stage1(q):
        for m in range(4):
            pair_copy(q, m).wait_recv()
        twin[q] = twin[q] + part[q, core]
        for n in (0, 2, 1, 3):
            near_copy(q, n).start()

    def stage2(q):
        u = here(q)
        near_copy(q, 0).wait_recv()
        near[q, 0] = near[q, 0] + twin[q, ring4(u, 1), 0:2]
        far_copy(q, 0).start()
        near_copy(q, 2).wait_recv()
        near[q, 2] = near[q, 2] + twin[q, ring4(u, -1), 2:4]
        far_copy(q, 1).start()

    def stage3(q):
        u = here(q)
        near_copy(q, 1).wait_recv()
        near_copy(q, 3).wait_recv()
        far_copy(q, 0).wait_recv()
        final[q, 0:2] = twin[q, u, 0:2] + near[q, 3] + far[q, 0]
        far_copy(q, 1).wait_recv()
        final[q, 2:4] = twin[q, u, 2:4] + near[q, 1] + far[q, 1]
        for s in (1, 2, 3):
            last_copy(q, s).start()

    def stage4(q):
        v = here(q + 1)
        for s in (1, 2, 3):
            last_copy(q, s).wait_recv()
        x_ref[:, q * W:(q + 1) * W] = final[q, v] + last[q, 1] + last[q, 2] + last[q, 3]

    def gram_steps(p):
        mine, half, parts, planes, gram = bufs[p]
        two_send, two_recv, part_send, part_recv, plane_send, plane_recv, back_send, back_recv = sems[p]
        deep = TILE * (p + 1)
        size = deep // CHIPS
        own = pl.ds(pl.multiple_of(core * deep, 8), deep)
        away = pl.ds(pl.multiple_of(other * deep, 8), deep)

        def pair(n):
            src, dst = (mine.at[away], half) if n == 0 else (gram.at[own], gram.at[own])
            return remote(src, dst, two_send.at[n], two_recv.at[n], twin_id)

        def chip_copy(i):
            there = lax.rem(chip + i, CHIPS)
            return remote(half.at[pl.ds(pl.multiple_of(there * size, 8), size)], parts.at[i],
                          part_send.at[i], part_recv.at[i], at_chip(i))

        def plane_copy(i, which):
            ref = planes.at[which]
            return remote(ref, ref, plane_send.at[i], plane_recv.at[i], at_plane(i))

        def piece(n):
            return pl.ds(pl.multiple_of(core * deep + n * size, 8), size)

        def back_copy(i, which):
            ref = gram.at[piece(which)]
            return remote(ref, ref, back_send.at[i], back_recv.at[i], at_chip(i))

        def loop(low, high, act):
            def one(i, carry):
                act(i)
                return carry
            lax.fori_loop(low, high, one, 0)

        def local():
            g = mm(x_ref[:, :deep], x_ref[:, p * TILE:(p + 1) * TILE], ((0,), (0,)))
            mine[0:deep, :] = g[:, :W]
            mine[deep:, :] = g[:, W:]
            pair(0).start()

        def to_chips():
            pair(0).wait_recv()
            half[...] = half[...] + mine[own, :]
            loop(1, CHIPS, lambda i: chip_copy(i).start())

        def to_planes():
            def add(i, total):
                chip_copy(i).wait_recv()
                return total + parts[i]
            planes[z] = lax.fori_loop(1, CHIPS, add, half[pl.ds(pl.multiple_of(chip * size, 8), size), :])
            loop(1, DEPTH, lambda i: plane_copy(i, z).start())

        def back():
            loop(1, DEPTH, lambda i: plane_copy(i, lax.rem(z + DEPTH - i, DEPTH)).wait_recv())
            total = planes[0]
            for i in range(1, DEPTH):
                total = total + planes[i]
            gram[piece(chip), :] = total
            loop(1, CHIPS, lambda i: back_copy(i, chip).start())

        def to_pair():
            loop(1, CHIPS, lambda i: back_copy(i, lax.rem(chip + CHIPS - i, CHIPS)).wait_recv())
            pair(1).start()

        def done():
            ref = gram.at[away]
            remote(ref, ref, two_send.at[1], two_recv.at[1], twin_id).wait_recv()
            s_ref[0:deep, p * TILE:p * TILE + W] = gram[0:deep, :]
            s_ref[0:deep, p * TILE + W:(p + 1) * TILE] = gram[deep:, :]

        def sent():
            pair(0).wait_send()
            pair(1).wait_send()
            loop(1, CHIPS, lambda i: chip_copy(i).wait_send())
            loop(1, DEPTH, lambda i: plane_copy(i, z).wait_send())
            loop(1, CHIPS, lambda i: back_copy(i, chip).wait_send())

        return local, to_chips, to_planes, back, to_pair, done, sent

    eye = (lax.broadcasted_iota(jnp.int32, (W, W), 0) == lax.broadcasted_iota(jnp.int32, (W, W), 1)).astype(F32)

    def solve(p):
        a, b, e = p * TILE, p * TILE + W, (p + 1) * TILE
        w = yield from factor(jnp.concatenate([s_ref[a:b, a:b], eye], axis=1))
        inv = w[:, W:]
        first = mm(x_ref[:, a:b], inv, ((1,), (1,)))
        out_ref[:, a:b] = first * scale
        u = mm(inv, s_ref[a:b, b:e], ((1,), (0,)))
        s_ref[b:e, b:e] = s_ref[b:e, b:e] - mm(u, u, ((0,), (0,)))
        w = yield from factor(jnp.concatenate([s_ref[b:e, b:e], eye], axis=1))
        inv2 = w[:, W:]
        second = mm(x_ref[:, b:e] - mm(first, u, ((1,), (0,))), inv2, ((1,), (1,)))
        out_ref[:, b:e] = second * scale
        if p == 0:
            x_ref[:, a:b] = first
            x_ref[:, b:e] = second
            u_ref[0:W, 0:W] = inv
            u_ref[0:W, W:] = jnp.zeros_like(inv)
            u_ref[W:, 0:W] = -mm(inv2, mm(u, inv, ((0,), (0,))), ((1,), (0,)))
            u_ref[W:, W:] = inv2

    def couple():
        u = mm(u_ref[...], s_ref[:TILE, TILE:], ((1,), (0,)))
        s_ref[TILE:, TILE:] = s_ref[TILE:, TILE:] - mm(u, u, ((0,), (0,)))
        x_ref[:, TILE:] = x_ref[:, TILE:] - mm(x_ref[:, :TILE], u, ((1,), (0,)))

    def run(*acts):
        for act in acts:
            act[0](*act[1:])

    for a in range(4):
        ring(0, a, 0)
    ring(1, 0, 0)
    fetch.wait()
    run((build, 0), (build, 1), (build, 2), (build, 3))
    for a in range(4):
        run((ring, 0, a, 1), (build, 4 + a))
    ring(1, 1, 0)
    build(8)
    for a in range(4):
        run((ring, 0, a, 2), (build, 9 + a))
    run((ring, 1, 2, 0), (ring, 1, 0, 1), (build, 13))
    run((ring, 0, 0, 3), (build, 14), (ring, 0, 1, 3), (build, 15))
    run((ring, 1, 3, 0), (ring, 1, 1, 1), (finish, 0), (ring, 1, 2, 1))
    compute_other(0)
    run((ring, 1, 3, 1), (ring, 1, 0, 2))
    compute_own(0)
    run((ring, 1, 1, 2), (stage1, 0), (stage1, 1), (ring, 1, 2, 2), (ring, 1, 3, 2))
    run((stage2, 0), (stage2, 1), (ring, 1, 0, 3), (ring, 1, 1, 3), (stage3, 0), (stage3, 1))
    finish(1)
    compute_other(1)
    run((stage4, 0), (stage4, 1))
    early, late = gram_steps(0), gram_steps(1)
    early[0]()
    compute_own(1)
    run((stage1, 2), (stage1, 3))
    early[1]()
    run((stage2, 2), (stage2, 3))
    early[2]()
    run((stage3, 2), (stage3, 3))
    early[3]()
    run((stage4, 2), (stage4, 3))
    late[0]()
    early[4]()
    late[1]()
    early[5]()
    for n, _ in enumerate(solve(0)):
        if n in (4, 8, 12):
            late[2 + n // 4 - 1]()
    late[5]()
    couple()
    for _ in solve(1):
        pass

    for p in range(2):
        for h in range(4):
            for a in range(2 if h == 3 else 4):
                for way in (0, 1):
                    hop(p, a + 2 if h == 3 and way == 1 else a, h, way).wait_send()
    for q in range(NQ):
        for n in range(4):
            pair_copy(q, n).wait_send()
            near_copy(q, n).wait_send()
        for n in range(2):
            far_copy(q, n).wait_send()
        for s in (1, 2, 3):
            last_copy(q, s).wait_send()
    early[6]()
    late[6]()


def basis_of(slot_of, tiles, panel, scale):
    dma = pltpu.SemaphoreType.DMA

    def gram_buffers(p):
        deep = TILE * (p + 1)
        size = deep // CHIPS
        return [VMEM((2 * deep, W), F32), VMEM((deep, W), F32), VMEM((CHIPS, size, W), F32),
                VMEM((DEPTH, size, W), F32), VMEM((2 * deep, W), F32)]

    gram_sems = [dma((2,)), dma((2,)), dma((CHIPS,)), dma((CHIPS,)), dma((DEPTH,)), dma((DEPTH,)),
                 dma((CHIPS,)), dma((CHIPS,))]
    return pl.pallas_call(
        lambda *refs: fused_kernel(scale, *refs),
        out_shape=jax.ShapeDtypeStruct((OWN, K), F32),
        in_specs=[
            pl.BlockSpec(memory_space=SMEM),
            pl.BlockSpec(memory_space=pl.ANY),
            pl.BlockSpec(memory_space=VMEM),
        ],
        out_specs=pl.BlockSpec(memory_space=VMEM),
        scratch_shapes=[
            VMEM((SLOTS, TILE, TILE), BF16),
            VMEM((NB, 2, 4, TILE, TILE), BF16),
            VMEM((2, DEPTH, TILE, TILE), BF16),
            VMEM((NQ, 2, 4, 4, OWN, W), F32),
            VMEM((NQ, 4, 4, OWN, W), F32),
            VMEM((NQ, 4, 2, OWN, W), F32),
            VMEM((NQ, 2, 2, OWN, W), F32),
            VMEM((NQ, 4, OWN, W), F32),
            VMEM((NQ, 4, OWN, W), F32),
            VMEM((OWN, K), F32),
            VMEM((K, K), F32),
            VMEM((TILE, TILE), F32),
            *gram_buffers(0),
            *gram_buffers(1),
            dma, dma((2, 2, 4, 4)), dma((2, 2, 4, 4)), dma((NQ, 4)), dma((NQ, 4)), dma((NQ, 4)), dma((NQ, 4)),
            dma((NQ, 2)), dma((NQ, 2)), dma((NQ, 4)), dma((NQ, 4)),
            *gram_sems,
            *gram_sems,
        ],
        compiler_params=pltpu.CompilerParams(
            vmem_limit_bytes=56 * 2**20, collective_id=0, has_side_effects=True),
        name="panel_basis",
    )(slot_of, tiles, panel)


def local(tiles, coords, counts, panel):
    where = coords[0, 0]
    position = where[:, 0] * NB + where[:, 1]
    slots = jnp.arange(SLOTS, dtype=jnp.int32)
    live = slots < counts[0, 0]
    match = (position[None, :] == jnp.arange(NB * NB, dtype=jnp.int32)[:, None]) & live[None, :]
    slot_of = jnp.min(jnp.where(match, slots[None, :], SLOTS), axis=1)
    scale = float((NB * TILE * DEPTH) ** 0.5)
    return basis_of(slot_of, tiles[0, 0], panel, scale)


def solution(mesh):
    placed = (
        P("row", "col", None, None, None),
        P("row", "col", None, None),
        P("row", "col"),
        P(("row", "col"), None),
    )
    return jax.shard_map(
        local, mesh=mesh, in_specs=placed, out_specs=P(("col", "row"), None), check_vma=False
    )
```

time: 780 us -> 101 us (0.13)
  waiting for transfers between devices: 583 us -> 0 us
  other arithmetic: 120 us -> 1.38 us
  Pallas kernels: 0 us -> 96.8 us
  matrix products: 24.6 us -> 0 us
  local copies, waits for them, and re-layouts: 17.4 us -> 1.57 us
  loops' own time: 15.8 us -> 0 us
  between operations: 15.9 us -> 0.67 us
    reduce_scatter x1 -> x0, waiting for transfers between devices: 280 us -> none  [local(): lax.psum_scatter(partial_sum, 'row', scatter_dimension=0, tiled=True)]
    psum x1 -> x0, waiting for transfers between devices: 259 us -> none  [local(): gram = lax.psum(local_gram, ('row', 'col'))]
    another operation x17 -> x0, other arithmetic: 118 us -> none  [the longest x14 78.8 us: local(): lower = jnp.linalg.cholesky(gram)]
    pallas_call x0 -> x1, Pallas kernels: none -> 96.8 us  [basis_of(): pl.pallas_call(lambda *refs: fused_kernel(scale, *refs), out_shape=jax.Sh...]
    all_gather x1 -> x0, waiting for transfers between devices: 43.1 us -> none  [local(): gathered = lax.all_gather(panel, 'col', axis=0, tiled=True)]
    dot_general x9 -> x0, matrix products: 21.1 us -> none  [the longest x8 18.1 us: add_tile(): lax.dot_general(single, rows_in, (((0,), (0,)), ((), ())), preferred_elem...]
    another operation x2 -> x0, loops' own time: 15.8 us -> none  [the longest x1 15.7 us: local(): partial_sum = lax.fori_loop(0, live_count, add_tile, start)]
    another operation x17 -> x0, local copies, waits for them, and re-layouts: 8.21 us -> none
  transfers between devices with their start and end apart: 3 -> 0, of which waited for: 3 -> 0; matrix products, arithmetic and copies ran while one was open for 0% -> 0% of each run, Pallas kernels for 0% -> 0%
where the time goes in v4:
time: 101 us; the launch traced here: 100 us
  Pallas kernels  96.8 us (96%)
  local copies, waits for them, and re-layouts  1.57 us (2%)
  other arithmetic  1.38 us (1%)
    pallas_call x1, Pallas kernels, basis_of(): pl.pallas_call(lambda *refs: fused_kernel(scale, *refs), out_shape=jax.Sh...  96.8 us

profile of v4, /device:TPU:1, one launch (start us, length us, event | category | flops | bytes accessed | tf_op | source)
XLA Modules:
  0.0 100.4 jit_solution(4145974449883737824)
XLA Ops:
  0.7 0.8 add_bitcast_fusion
  1.4 0.6 select_reduce_fusion.refs_0_
  2.0 96.8 %panel_basis.1 = f32[64,512]{1,0:T(8,128)} custom-call(s32[64]{0:T(128)} %select_reduce_fusion.refs_0_, bf16[48,256,256]{2,1,0:T(8,128)(2,1)} %bitcast.6, bf16[256,512]{1,0:T(8,128)(2,1)} %refs_2_.1), custom_call_target="tpu_custom_call" | custom-call | tf_op jit(solution)/shard_map/panel_basis/pallas_call | solution.py:425
  98.8 1.6 %copy.7 = f32[64,512]{1,0:T(8,128)} copy(f32[64,512]{1,0:T(8,128)} %panel_basis.1) | data formatting | bytes 262144
  (1 shorter events, 0.0 us)

commit v5 on v4

--- a/solution.py
+++ b/solution.py
@@ -73,12 +73,12 @@
     return jnp.concatenate(rows, axis=0)
 
 
-def fused_kernel(scale, slot_ref, tiles_hbm, panel_ref, out_ref, tiles_ref, at_ref, pan, part, twin, near, far, final,
+def fused_kernel(scale, coords_ref, count_ref, tiles_hbm, panel_hbm, out_ref, slot_vec, slot_ref, tiles_ref, at_ref, pan, part, twin, near, far, final,
                  last, x_ref, s_ref, u_ref, *rest):
     bufs = (rest[0:5], rest[5:10])
-    (tile_sem, ring_send, ring_recv, pair_send, pair_recv, near_send, near_recv, far_send, far_recv,
-     last_send, last_recv) = rest[10:21]
-    sems = (rest[21:29], rest[29:37])
+    (slot_sem, panel_sem, tile_sem, ring_send, ring_recv, pair_send, pair_recv, near_send, near_recv, far_send, far_recv,
+     last_send, last_recv) = rest[10:23]
+    sems = (rest[23:31], rest[31:39])
     row, z = lax.axis_index("row"), lax.axis_index("col")
     core, chip = row % 2, row // 2
     x, y = chip % 4, chip // 4
@@ -107,6 +107,9 @@
             pl.semaphore_signal(barrier, inc=1, device_id=device_of(i), device_id_type=MESH)
             return carry
         return one
+
+    def block_rows(block, start, count):
+        return pl.ds(pl.multiple_of(block * TILE + start, 64), count)
 
     barrier = pltpu.get_barrier_semaphore()
     lax.fori_loop(1, DEPTH, hello(at_plane), 0)
@@ -114,8 +117,20 @@
     pl.semaphore_signal(barrier, inc=1, device_id=twin_id, device_id_type=MESH)
     fetch = pltpu.make_async_copy(tiles_hbm, tiles_ref, tile_sem)
     fetch.start()
-    for p in range(2):
-        pan[p, z] = panel_ref[:, p * TILE:(p + 1) * TILE]
+    own_panel = [pltpu.make_async_copy(panel_hbm.at[:, pl.ds(p * TILE, TILE)], pan.at[p, block_rows(z, 0, TILE)],
+                                       panel_sem.at[p]) for p in range(2)]
+    for copy in own_panel:
+        copy.start()
+
+    position = coords_ref[0:1, :] * NB + coords_ref[1:2, :]
+    slot = lax.broadcasted_iota(jnp.int32, (NB * NB, SLOTS), 1)
+    match = (position == lax.broadcasted_iota(jnp.int32, (NB * NB, SLOTS), 0)) & (slot < count_ref[0, 0])
+    first = jnp.min(jnp.where(match, slot, SLOTS), axis=1, keepdims=True)
+    slot_vec[...] = jnp.broadcast_to(first, (NB * NB, W))
+    to_scalars = pltpu.make_async_copy(slot_vec, slot_ref, slot_sem)
+    to_scalars.start()
+    for copy in own_panel:
+        copy.wait()
     pl.semaphore_wait(barrier, DEPTH - 1 + CHIPS - 1 + 1)
 
     def remote(src, dst, send, recv, peer):
@@ -123,7 +138,7 @@
             src_ref=src, dst_ref=dst, send_sem=send, recv_sem=recv, device_id=peer, device_id_type=MESH)
 
     def ring_copy(p, a, h, way, block):
-        ref = pan.at[p, block, pl.ds(a * 64, 64)]
+        ref = pan.at[p, block_rows(block, a * 64, 64)]
         return remote(ref, ref, ring_send.at[way, p, a, h], ring_recv.at[way, p, a, h], up if way == 0 else down)
 
     def hop(p, a, h, way):
@@ -150,14 +165,14 @@
         b, first = part_of // 2, part_of % 2 * 4
 
         def one(i, carry):
-            n = slot_ref[b * NB + i]
+            n = slot_ref[b * NB + i, 0]
             tile = tiles_ref[jnp.minimum(n, SLOTS - 1)]
             tile = jnp.where(n < SLOTS, tile, jnp.zeros_like(tile)).T
             for xl in range(2):
                 for c in range(2):
                     at = (xl * 2 + c) * 64
                     to = pl.multiple_of((2 * (i % 2) + xl) * 64, 64)
-                    at_ref[b, c, i // 2, pl.ds(to, 64), :] = tile[at:at + 64, :]
+                    at_ref[c, i // 2, pl.ds(to, 64), b * TILE:(b + 1) * TILE] = tile[at:at + 64, :]
             return carry
 
         lax.fori_loop(first, first + 4, one, 0)
@@ -170,27 +185,19 @@
         return remote(src, dst, pair_send.at[q, m], pair_recv.at[q, m], twin_id)
 
     def multiply(p, c, m):
-        total = jnp.dot(at_ref[0, c, m], pan[p, 0], preferred_element_type=F32)
-        for b in range(1, NB):
-            total += jnp.dot(at_ref[b, c, m], pan[p, b], preferred_element_type=F32)
+        total = jnp.dot(at_ref[c, m], pan[p], preferred_element_type=F32)
         for xx in range(4):
             piece = total[xx * 64:(xx + 1) * 64, :]
             part[2 * p, c, xx, m] = piece[:, :W]
             part[2 * p + 1, c, m, xx] = piece[:, W:]
 
-    def compute_other(p):
-        def one(m, carry):
-            multiply(p, other, m)
-            pair_copy(2 * p, m).start()
-            pair_copy(2 * p + 1, m).start()
-            return carry
-        lax.fori_loop(0, 4, one, 0)
-
-    def compute_own(p):
-        def one(m, carry):
-            multiply(p, core, m)
-            return carry
-        lax.fori_loop(0, 4, one, 0)
+    def other_rows(p, m):
+        multiply(p, other, m)
+        pair_copy(2 * p, m).start()
+        pair_copy(2 * p + 1, m).start()
+
+    def own_rows(p, m):
+        multiply(p, core, m)
 
     def here(q):
         return x if q % 2 == 0 else y
@@ -275,7 +282,7 @@
             lax.fori_loop(low, high, one, 0)
 
         def local():
-            g = mm(x_ref[:, :deep], x_ref[:, p * TILE:(p + 1) * TILE], ((0,), (0,)))
+            g = stacked(x_ref[:, :deep], x_ref[:, p * TILE:(p + 1) * TILE])
             mine[0:deep, :] = g[:, :W]
             mine[deep:, :] = g[:, W:]
             pair(0).start()
@@ -310,14 +317,18 @@
             s_ref[0:deep, p * TILE:p * TILE + W] = gram[0:deep, :]
             s_ref[0:deep, p * TILE + W:(p + 1) * TILE] = gram[deep:, :]
 
-        def sent():
+        def sent_there():
             pair(0).wait_send()
-            pair(1).wait_send()
             loop(1, CHIPS, lambda i: chip_copy(i).wait_send())
             loop(1, DEPTH, lambda i: plane_copy(i, z).wait_send())
+
+        def sent_back():
             loop(1, CHIPS, lambda i: back_copy(i, chip).wait_send())
 
-        return local, to_chips, to_planes, back, to_pair, done, sent
+        def sent_pair():
+            pair(1).wait_send()
+
+        return local, to_chips, to_planes, back, to_pair, done, sent_there, sent_back, sent_pair
 
     eye = (lax.broadcasted_iota(jnp.int32, (W, W), 0) == lax.broadcasted_iota(jnp.int32, (W, W), 1)).astype(F32)
 
@@ -350,56 +361,14 @@
         for act in acts:
             act[0](*act[1:])
 
-    for a in range(4):
-        ring(0, a, 0)
-    ring(1, 0, 0)
-    fetch.wait()
-    run((build, 0), (build, 1), (build, 2), (build, 3))
-    for a in range(4):
-        run((ring, 0, a, 1), (build, 4 + a))
-    ring(1, 1, 0)
-    build(8)
-    for a in range(4):
-        run((ring, 0, a, 2), (build, 9 + a))
-    run((ring, 1, 2, 0), (ring, 1, 0, 1), (build, 13))
-    run((ring, 0, 0, 3), (build, 14), (ring, 0, 1, 3), (build, 15))
-    run((ring, 1, 3, 0), (ring, 1, 1, 1), (finish, 0), (ring, 1, 2, 1))
-    compute_other(0)
-    run((ring, 1, 3, 1), (ring, 1, 0, 2))
-    compute_own(0)
-    run((ring, 1, 1, 2), (stage1, 0), (stage1, 1), (ring, 1, 2, 2), (ring, 1, 3, 2))
-    run((stage2, 0), (stage2, 1), (ring, 1, 0, 3), (ring, 1, 1, 3), (stage3, 0), (stage3, 1))
-    finish(1)
-    compute_other(1)
-    run((stage4, 0), (stage4, 1))
-    early, late = gram_steps(0), gram_steps(1)
-    early[0]()
-    compute_own(1)
-    run((stage1, 2), (stage1, 3))
-    early[1]()
-    run((stage2, 2), (stage2, 3))
-    early[2]()
-    run((stage3, 2), (stage3, 3))
-    early[3]()
-    run((stage4, 2), (stage4, 3))
-    late[0]()
-    early[4]()
-    late[1]()
-    early[5]()
-    for n, _ in enumerate(solve(0)):
-        if n in (4, 8, 12):
-            late[2 + n // 4 - 1]()
-    late[5]()
-    couple()
-    for _ in solve(1):
-        pass
-
-    for p in range(2):
-        for h in range(4):
-            for a in range(2 if h == 3 else 4):
-                for way in (0, 1):
-                    hop(p, a + 2 if h == 3 and way == 1 else a, h, way).wait_send()
-    for q in range(NQ):
+    def ring_sent():
+        for p in range(2):
+            for h in range(4):
+                for a in range(2 if h == 3 else 4):
+                    for way in (0, 1):
+                        hop(p, a + 2 if h == 3 and way == 1 else a, h, way).wait_send()
+
+    def rows_sent(q):
         for n in range(4):
             pair_copy(q, n).wait_send()
             near_copy(q, n).wait_send()
@@ -407,11 +376,67 @@
             far_copy(q, n).wait_send()
         for s in (1, 2, 3):
             last_copy(q, s).wait_send()
-    early[6]()
+
+    early, late = gram_steps(0), gram_steps(1)
+
+    for a in range(4):
+        ring(0, a, 0)
+    run((ring, 1, 0, 0), (ring, 1, 1, 0))
+    fetch.wait()
+    to_scalars.wait()
+    run((build, 0), (build, 1), (build, 2), (build, 3))
+    for a in range(4):
+        run((ring, 0, a, 1), (build, 4 + a))
+    run((ring, 1, 2, 0), (ring, 1, 3, 0), (build, 8))
+    for a in range(4):
+        run((ring, 0, a, 2), (build, 9 + a))
+    run((ring, 1, 0, 1), (ring, 1, 1, 1), (build, 13))
+    run((ring, 0, 0, 3), (build, 14), (ring, 0, 1, 3), (build, 15))
+    run((ring, 1, 2, 1), (ring, 1, 3, 1), (finish, 0))
+    for m in range(4):
+        other_rows(0, m)
+    for m in range(4):
+        run((own_rows, 0, m), (ring, 1, m, 2))
+    run((stage1, 0), (stage1, 1), (ring, 1, 0, 3), (ring, 1, 1, 3), (stage2, 0), (stage2, 1))
+    finish(1)
+    for m in range(4):
+        other_rows(1, m)
+    run((stage3, 0), (stage3, 1))
+    for m in range(4):
+        own_rows(1, m)
+    run((stage1, 2), (stage1, 3))
+    run((stage4, 0), (stage4, 1))
+    early[0]()
+    early[1]()
+    run((stage2, 2), (stage2, 3))
+    early[2]()
+    run((stage3, 2), (stage3, 3))
+    run((stage4, 2), (stage4, 3))
+    late[0]()
+    late[1]()
+    early[3]()
+    ring_sent()
+    early[4]()
+    late[2]()
+    early[5]()
+    for n, _ in enumerate(solve(0)):
+        if n == 8:
+            late[3]()
+    for q in range(NQ):
+        rows_sent(q)
+    for n in (6, 7, 8):
+        early[n]()
     late[6]()
-
-
-def basis_of(slot_of, tiles, panel, scale):
+    late[4]()
+    late[7]()
+    late[5]()
+    couple()
+    for _ in solve(1):
+        pass
+    late[8]()
+
+
+def basis_of(coords, count, tiles, panel, scale):
     dma = pltpu.SemaphoreType.DMA
 
     def gram_buffers(p):
@@ -426,15 +451,18 @@
         lambda *refs: fused_kernel(scale, *refs),
         out_shape=jax.ShapeDtypeStruct((OWN, K), F32),
         in_specs=[
+            pl.BlockSpec(memory_space=VMEM),
             pl.BlockSpec(memory_space=SMEM),
-            pl.BlockSpec(memory_space=pl.ANY),
-            pl.BlockSpec(memory_space=VMEM),
+            pl.BlockSpec(memory_space=pltpu.HBM),
+            pl.BlockSpec(memory_space=pltpu.HBM),
         ],
         out_specs=pl.BlockSpec(memory_space=VMEM),
         scratch_shapes=[
+            VMEM((NB * NB, W), jnp.int32),
+            SMEM((NB * NB, W), jnp.int32),
             VMEM((SLOTS, TILE, TILE), BF16),
-            VMEM((NB, 2, 4, TILE, TILE), BF16),
-            VMEM((2, DEPTH, TILE, TILE), BF16),
+            VMEM((2, 4, TILE, NB * TILE), BF16),
+            VMEM((2, NB * TILE, TILE), BF16),
             VMEM((NQ, 2, 4, 4, OWN, W), F32),
             VMEM((NQ, 4, 4, OWN, W), F32),
             VMEM((NQ, 4, 2, OWN, W), F32),
@@ -446,7 +474,7 @@
             VMEM((TILE, TILE), F32),
             *gram_buffers(0),
             *gram_buffers(1),
-            dma, dma((2, 2, 4, 4)), dma((2, 2, 4, 4)), dma((NQ, 4)), dma((NQ, 4)), dma((NQ, 4)), dma((NQ, 4)),
+            dma, dma((2,)), dma, dma((2, 2, 4, 4)), dma((2, 2, 4, 4)), dma((NQ, 4)), dma((NQ, 4)), dma((NQ, 4)), dma((NQ, 4)),
             dma((NQ, 2)), dma((NQ, 2)), dma((NQ, 4)), dma((NQ, 4)),
             *gram_sems,
             *gram_sems,
@@ -454,18 +482,12 @@
         compiler_params=pltpu.CompilerParams(
             vmem_limit_bytes=56 * 2**20, collective_id=0, has_side_effects=True),
         name="panel_basis",
-    )(slot_of, tiles, panel)
+    )(coords, count, tiles, panel)
 
 
 def local(tiles, coords, counts, panel):
-    where = coords[0, 0]
-    position = where[:, 0] * NB + where[:, 1]
-    slots = jnp.arange(SLOTS, dtype=jnp.int32)
-    live = slots < counts[0, 0]
-    match = (position[None, :] == jnp.arange(NB * NB, dtype=jnp.int32)[:, None]) & live[None, :]
-    slot_of = jnp.min(jnp.where(match, slots[None, :], SLOTS), axis=1)
     scale = float((NB * TILE * DEPTH) ** 0.5)
-    return basis_of(slot_of, tiles[0, 0], panel, scale)
+    return basis_of(coords[0, 0].T, counts, tiles[0, 0], panel, scale)
 
 
 def solution(mesh):

time: 101 us -> 96.8 us (0.958)
  Pallas kernels: 96.8 us -> 94.5 us
  other arithmetic: 1.38 us -> 0 us
    pallas_call x1, Pallas kernels: 96.8 us -> 94.5 us  [basis_of(): pl.pallas_call(lambda *refs: fused_kernel(scale, *refs), out_shape=jax.Sh...]
where the time goes in v5:
time: 96.8 us; the launch traced here: 96.7 us
  Pallas kernels  94.5 us (98%)
  local copies, waits for them, and re-layouts  1.57 us (2%)
    pallas_call x1, Pallas kernels, basis_of(): pl.pallas_call(lambda *refs: fused_kernel(scale, *refs), out_shape=jax.Sh...  94.5 us

profile of v5, /device:TPU:1, one launch (start us, length us, event | category | flops | bytes accessed | tf_op | source)
XLA Modules:
  0.0 96.7 jit_solution(8254269426970919649)
XLA Ops:
  0.7 94.5 %panel_basis.1 = f32[64,512]{1,0:T(8,128)} custom-call(s32[2,48]{1,0:T(2,128)} %bitcast.5, s32[1,1]{1,0:T(1,128)S(6)} %copy.6.refs_1_, bf16[48,256,256]{2,1,0:T(8,128)(2,1)} %bitcast.4, bf16[256,512]{1,0:T(8,128)(2,1)} %refs_3_.1), custom_call_target="tpu_custom_call" | custom-call | tf_op jit(solution)/shard_map/panel_basis/pallas_call | solution.py:450
  95.1 1.6 %copy.7 = f32[64,512]{1,0:T(8,128)} copy(f32[64,512]{1,0:T(8,128)} %panel_basis.1) | data formatting | bytes 262144

commit v6 on v5

--- a/solution.py
+++ b/solution.py
@@ -381,18 +381,20 @@
 
     for a in range(4):
         ring(0, a, 0)
-    run((ring, 1, 0, 0), (ring, 1, 1, 0))
+    ring(1, 0, 0)
     fetch.wait()
     to_scalars.wait()
     run((build, 0), (build, 1), (build, 2), (build, 3))
     for a in range(4):
         run((ring, 0, a, 1), (build, 4 + a))
-    run((ring, 1, 2, 0), (ring, 1, 3, 0), (build, 8))
+    run((ring, 1, 1, 0), (build, 8))
     for a in range(4):
         run((ring, 0, a, 2), (build, 9 + a))
-    run((ring, 1, 0, 1), (ring, 1, 1, 1), (build, 13))
+    run((ring, 1, 2, 0), (ring, 1, 3, 0), (build, 13))
     run((ring, 0, 0, 3), (build, 14), (ring, 0, 1, 3), (build, 15))
-    run((ring, 1, 2, 1), (ring, 1, 3, 1), (finish, 0))
+    for a in range(4):
+        ring(1, a, 1)
+    finish(0)
     for m in range(4):
         other_rows(0, m)
     for m in range(4):
@@ -410,24 +412,26 @@
     early[1]()
     run((stage2, 2), (stage2, 3))
     early[2]()
+    rows_sent(0)
+    rows_sent(1)
     run((stage3, 2), (stage3, 3))
     run((stage4, 2), (stage4, 3))
     late[0]()
     late[1]()
+    rows_sent(2)
+    rows_sent(3)
+    ring_sent()
     early[3]()
-    ring_sent()
     early[4]()
     late[2]()
     early[5]()
     for n, _ in enumerate(solve(0)):
         if n == 8:
             late[3]()
-    for q in range(NQ):
-        rows_sent(q)
+    late[4]()
     for n in (6, 7, 8):
         early[n]()
     late[6]()
-    late[4]()
     late[7]()
     late[5]()
     couple()

time: 96.8 us -> 96.1 us (level)
  no operation moved by 1% of the time
where the time goes in v6:
time: 96.1 us; the launch traced here: 95.9 us
  Pallas kernels  93.7 us (98%)
  local copies, waits for them, and re-layouts  1.57 us (2%)
    pallas_call x1, Pallas kernels, basis_of(): pl.pallas_call(lambda *refs: fused_kernel(scale, *refs), out_shape=jax.Sh...  93.7 us

profile of v6, /device:TPU:1, one launch (start us, length us, event | category | flops | bytes accessed | tf_op | source)
XLA Modules:
  0.0 95.9 jit_solution(14010184493719316983)
XLA Ops:
  0.7 93.7 %panel_basis.1 = f32[64,512]{1,0:T(8,128)} custom-call(s32[2,48]{1,0:T(2,128)} %bitcast.5, s32[1,1]{1,0:T(1,128)S(6)} %copy.6.refs_1_, bf16[48,256,256]{2,1,0:T(8,128)(2,1)} %bitcast.4, bf16[256,512]{1,0:T(8,128)(2,1)} %refs_3_.1), custom_call_target="tpu_custom_call" | custom-call | tf_op jit(solution)/shard_map/panel_basis/pallas_call | solution.py:454
  94.4 1.6 %copy.7 = f32[64,512]{1,0:T(8,128)} copy(f32[64,512]{1,0:T(8,128)} %panel_basis.1) | data formatting | bytes 262144
